TPU v7x, 32 devices: a whole 2x2x4 slice. The times are simulated.
32 devices in a mesh: gx: 2 (over y), gy: 16 (over z, x, core).
Axes of the slice: x: 2, y: 2, z: 4, core: 2. Of those that a mesh axis runs over, the one named last changes fastest.
Arguments:
- tokens: bfloat16 [4096, 768], P(('gx', 'gy')), may hold values from -6 to 6
- timesteps: int32 [64], P(('gx', 'gy')), may hold values from 0 to 999
- lengths: int32 [32, 2], P(('gx', 'gy')), may hold values from 1 to 96, 128 in all within a row
- routes: int32 [4096, 2], P(('gx', 'gy')), may hold values from 0 to 7, all different within a row; in each aligned block of 128 rows (0 to 127, 128 to 255, ...) at most 64 rows name the same one
- cotangent: bfloat16 [4096, 768], P(('gx', 'gy')), may hold values from -6 to 6
- w_ada: bfloat16 [768, 4608], P(('gx', 'gy')), may hold values from -0.625 to 0.625
- w_qkv: bfloat16 [768, 2304], P(('gx', 'gy')), may hold values from -0.21875 to 0.21875
- w_out: bfloat16 [768, 768], P(('gx', 'gy')), may hold values from -0.875 to 0.875
- w_fc1: bfloat16 [768, 3072], P(('gx', 'gy')), may hold values from -0.21875 to 0.21875
- w_fc2: bfloat16 [3072, 768], P(('gx', 'gy')), may hold values from -0.109375 to 0.109375
- w_router: bfloat16 [768, 8], P(('gx', 'gy')), may hold values from -0.15625 to 0.15625
- e_fc1: bfloat16 [8, 768, 3072], P('gx', 'gy'), may hold values from -0.21875 to 0.21875
- e_fc2: bfloat16 [8, 3072, 768], P('gx', 'gy'), may hold values from -0.4375 to 0.4375
Outputs:
- output: bfloat16 [4096, 768], P(('gx', 'gy'))
- d_tokens: float32 [4096, 768], P(('gx', 'gy'))
- d_w_ada: float32 [768, 4608], P(('gx', 'gy'))
- d_w_qkv: float32 [768, 2304], P(('gx', 'gy'))
- d_w_out: float32 [768, 768], P(('gx', 'gy'))
- d_w_fc1: float32 [768, 3072], P(('gx', 'gy'))
- d_w_fc2: float32 [3072, 768], P(('gx', 'gy'))
- d_w_router: float32 [768, 8], P(('gx', 'gy'))
- d_e_fc1: float32 [8, 768, 3072], P('gx', 'gy')
- d_e_fc2: float32 [8, 3072, 768], P('gx', 'gy')
Inputs may be any that keep to these rules, and one draw needn't show every extreme that they name: `lengths`: each device's row sums to 128; no item has more than 96 patches. `routes`: each row names two different experts. Among the rows of one device no expert is named more than 64 times; some device's rows name some expert exactly 64 times.
All inputs are finite; a program needn't handle non-finite values.
Results may differ from a plain program's by a relative error of at most 0.028.
Values may be sent and summed in bfloat16 or wider, within the bound.
A program may use at most 192 MiB of HBM per device.

v0:
```python
import functools
import math

import jax
import jax.numpy as jnp
from jax import lax
from jax.experimental import pallas as pl
from jax.experimental.pallas import tpu as pltpu
from jax.sharding import PartitionSpec as P

HEADS = 12
CAP = 64
MESH = pl.DeviceIdType.MESH
ANY = pl.ANY
VMEM = pltpu.VMEM
DMA = pltpu.SemaphoreType.DMA
LINE = (1, 3, 2)

precise = lax.Precision.HIGHEST
layer_epsilon = 1e-06


def place():
    gy = lax.axis_index("gy")
    return lax.axis_index("gx"), gy // 4, (gy // 2) % 2, gy % 2


def device(y, z, x, c):
    return (y, 4 * z + 2 * x + c)


def chip(y, z, x):
    return 8 * y + 2 * z + x


def meet(partners):
    barrier = pltpu.get_barrier_semaphore()
    for partner in partners:
        pl.semaphore_signal(barrier, inc=1, device_id=partner, device_id_type=MESH)
    pl.semaphore_wait(barrier, len(partners))


def cross_partners(here):
    y, z, x, c = here
    return [device(y, (z + step) % 4, x, c) for step in LINE] + [
        device(1 - y, z, x, c),
        device(y, z, 1 - x, c),
    ]


def remote(source, target, send, recv, to):
    return pltpu.make_async_remote_copy(
        src_ref=source, dst_ref=target, send_sem=send, recv_sem=recv, device_id=to, device_id_type=MESH
    )


class Gather:
    def __init__(self, here, y_first, own, slot, send, recv, pair=None):
        self.here, self.y_first, self.own, self.slot = here, y_first, own, slot
        self.send, self.recv, self.pair, self.started = send, recv, pair, []

    def copy(self, source, number, recv, to):
        sent = remote(source, self.slot(number), self.send.at[len(self.started)], recv.at[number], to)
        sent.start()
        self.started.append(sent)

    def forward(self, source, number, to_y, to_x, to_pair=True):
        y, z, x, c = self.here
        if to_y:
            self.copy(source, number, self.recv, device(1 - y, z, x, c))
        if to_x:
            self.copy(source, number, self.recv, device(y, z, 1 - x, c))
        if to_pair and self.pair is not None:
            self.copy(source, number, self.pair, device(y, z, x, 1 - c))

    def arrive(self, number, recv=None):
        recv = self.recv if recv is None else recv
        block = self.slot(number)
        remote(block, block, self.send.at[0], recv.at[number], device(*self.here)).wait_recv()
        return block

    def start_line(self, step):
        y, z, x, c = self.here
        self.copy(self.own, chip(y, z, x), self.recv, device(y, (z + step) % 4, x, c))

    def start_first(self):
        y, z, x, c = self.here
        self.forward(self.own, chip(y, z, x), self.y_first, not self.y_first)

    def start_last(self):
        y, z, x, c = self.here
        self.forward(self.own, chip(y, z, x), not self.y_first, self.y_first, False)

    def line_first(self, step):
        y, z, x, c = self.here
        number = chip(y, (z + step) % 4, x)
        self.forward(self.arrive(number), number, self.y_first, not self.y_first)

    def line_last(self, step):
        y, z, x, c = self.here
        number = chip(y, (z + step) % 4, x)
        self.forward(self.slot(number), number, not self.y_first, self.y_first, False)

    def second(self, step):
        y, z, x, c = self.here
        if self.y_first:
            number = chip(1 - y, (z + step) % 4, x)
        else:
            number = chip(y, (z + step) % 4, 1 - x)
        self.forward(self.arrive(number), number, not self.y_first, self.y_first)

    def third(self, step):
        y, z, x, c = self.here
        for other in (0, 1):
            if self.y_first:
                number = chip(y if other == 0 else 1 - y, (z + step) % 4, 1 - x)
            else:
                number = chip(1 - y, (z + step) % 4, x if other == 0 else 1 - x)
            self.forward(self.arrive(number), number, False, False)

    def finish(self):
        for sent in self.started:
            sent.wait_send()
        if self.pair is not None:
            for number in range(16):
                self.arrive(number, self.pair)


def gather_start(gathers):
    for gather in gathers:
        gather.start_first()
    for gather in gathers:
        gather.start_line(1)
        gather.start_line(3)
    for gather in gathers:
        gather.start_last()
    for gather in gathers:
        gather.start_line(2)


def gather_line(gathers, step):
    for gather in gathers:
        gather.line_first(step)
    for gather in gathers:
        gather.line_last(step)


def gather_second(gathers, step):
    for gather in gathers:
        gather.second(step)


def gather_third(gathers, step):
    for gather in gathers:
        gather.third(step)


def gather_all(gathers, between=None):
    gather_start(gathers)
    gather_second(gathers, 0)
    for step in LINE:
        gather_line(gathers, step)
        gather_second(gathers, step)
    if between is not None:
        between()
    for step in (0,) + LINE:
        gather_third(gathers, step)
    for gather in gathers:
        gather.finish()


class Scatter:
    def __init__(self, here, y_first, part, got, send, recv):
        self.here, self.y_first, self.part, self.got = here, y_first, part, got
        self.send, self.recv, self.started = send, recv, []

    def number(self, a, b, step):
        y, z, x, c = self.here
        flip_y, flip_x = (a, b) if self.y_first else (b, a)
        return chip(1 - y if flip_y else y, (z + step) % 4, 1 - x if flip_x else x)

    def toward(self, second):
        y, z, x, c = self.here
        return device(1 - y, z, x, c) if self.y_first != second else device(y, z, 1 - x, c)

    def copy(self, source, index, to):
        sent = remote(source, self.got(index), self.send.at[len(self.started)], self.recv.at[index], to)
        sent.start()
        self.started.append(sent)

    def arrive(self, index):
        block = self.got(index)
        remote(block, block, self.send.at[0], self.recv.at[index], device(*self.here)).wait_recv()
        return block

    def first(self, step):
        for b in (1, 0):
            self.copy(self.part(self.number(1, b, step)), 4 * b + step, self.toward(False))

    def add(self, number, index):
        block, mine = self.arrive(index), self.part(number)
        total = mine[...].astype(jnp.float32) + block[...].astype(jnp.float32)
        mine[...] = total.astype(mine.dtype)

    def one(self, b, step):
        number = self.number(0, b, step)
        self.add(number, 4 * b + step)
        if b == 1:
            self.copy(self.part(number), 8 + step, self.toward(True))

    def two(self, step):
        y, z, x, c = self.here
        number = self.number(0, 0, step)
        self.add(number, 8 + step)
        if step:
            self.copy(self.part(number), 11 + step, device(y, (z + step) % 4, x, c))

    def total(self):
        result = self.part(self.number(0, 0, 0))[...].astype(jnp.float32)
        for step in (1, 2, 3):
            result = result + self.arrive(11 + step)[...].astype(jnp.float32)
        return result

    def finish(self):
        for sent in self.started:
            sent.wait_send()


def scatter_all(scatters, between):
    order = (2, 1, 3, 0)
    for scatter in scatters:
        scatter.first(order[0])
    for scatter in scatters:
        scatter.first(order[1])
    for turn, step in enumerate(order):
        for scatter in scatters:
            scatter.one(1, step)
        for scatter in scatters:
            scatter.one(0, step)
        if turn + 2 < 4:
            for scatter in scatters:
                scatter.first(order[turn + 2])
        for scatter in scatters:
            scatter.two(step)
        between(turn)


def nt(a, b):
    return lax.dot_general(a, b, (((1,), (1,)), ((), ())), preferred_element_type=jnp.float32)


def tn(a, b):
    return lax.dot_general(a, b, (((0,), (0,)), ((), ())), preferred_element_type=jnp.float32)


def nn(a, b):
    return jnp.dot(a, b, preferred_element_type=jnp.float32)


def low(value):
    return value.astype(jnp.bfloat16)


def wide_float(value):
    return value.astype(jnp.float32)


def norm(values):
    centred = values - jnp.mean(values, axis=-1, keepdims=True)
    scale = lax.rsqrt(jnp.mean(centred * centred, axis=-1, keepdims=True) + layer_epsilon)
    return centred * scale, scale


def norm_back(grad, normed, scale):
    pulled = grad - jnp.mean(grad, axis=-1, keepdims=True) - normed * jnp.mean(grad * normed, axis=-1, keepdims=True)
    return scale * pulled


def item_mask(lengths, shape):
    return lax.broadcasted_iota(jnp.int32, shape, 0) >= lengths[0, 0]


def choices(routes, square):
    square[...] = jnp.zeros_like(square)
    square[0 : routes.shape[0], :] = wide_float(routes[...])
    named = square[...].T
    lane = wide_float(lax.broadcasted_iota(jnp.int32, (1, 128), 1))
    return (named[:, 0:1] == lane) | (named[:, 1:2] == lane)


def own_modulation(here, mod, item, half, part):
    y, z, x, c = here
    model = item.shape[1]
    first = 8 * y + 4 * x + 2 * c
    at = slice(part * model, (part + 1) * model)
    return jnp.where(item, mod[half, pl.ds(first + 1, 1), at], mod[half, pl.ds(first, 1), at])


def head_lanes():
    lane = lax.broadcasted_iota(jnp.int32, (1, 128), 1)
    return lane < 64, [low(wide_float(lane < 64)), low(wide_float(lane >= 64))]


def front_kernel(
    lengths, tokens, cotangent, routes, cond, w_ada, w_qkv, w_out, w_router, w_fc1, e1, e2, f2,
    w1, w1s, w2, w2s, qkv_w, out_w, conds, mod, mixed, grad, gates, attn_in, qkv, probs, attn_low, attn_proj, middle, chance,
    square, f1, s_got, s_rows, q_full, o_full, q_fold, o_fold, q_stage, o_stage, q_block, o_block, c_buf, part, sib, z_part, z_got, xy_part, xy_got,
    pre_send, pre_recv, g_send, g_recv, g_pair, a_send, a_recv, a_pair_send, a_pair, b_send, b_recv, b_pair, l_sem, d_send, d_recv,
    c_send, c_recv, m_send, m_recv,
):
    here = y, z, x, c = place()
    me, k, gy = chip(y, z, x), 2 * z + x, 4 * z + 2 * x + c
    rows, model = w_out.shape
    others = [(dy, dz, dx) for dy in (0, 1) for dz in (0, 1, 2, 3) for dx in (0, 1) if (dy, dz, dx) != (0, 0, 0)]
    spot = lambda dy, dz, dx: (1 - y if dy else y, (z + dz) % 4, 1 - x if dx else x)
    sibling = device(y, z, x, 1 - c)
    peers = [(*spot(dy, dz, dx), c if same else 1 - c) for same in (True, False) for dy, dz, dx in [(0, 0, 0)] + others]
    peers = peers[1:]
    meet([device(*peer) for peer in peers])

    started = []

    def go(copy):
        copy.start()
        started.append(copy)

    number = 2 * me + c
    for i, peer in enumerate(peers):
        go(remote(cond.at[2 * chip(*peer[:3]) + peer[3]], c_buf.at[number], c_send.at[i], c_recv.at[number], device(*peer)))

    mine = pl.ds(pl.multiple_of(rows * c, 8), rows)
    square[...] = jnp.zeros_like(square)
    square[0 : w_router.shape[0], 0:rows] = wide_float(w_router[...])
    router = square[...].T[:rows]
    for w, fold, stage, i in ((w_qkv, q_fold, q_stage, 0), (w_out, o_fold, o_stage, 1)):
        cut = w.shape[1] // 2
        for h in (0, 1):
            fold[h, :, :cut] = wide_float(w[:, h * cut : (h + 1) * cut])
            if i:
                fold[h, :, cut:] = router
        go(remote(fold.at[1 - c], stage.at[mine, :], pre_send.at[i], pre_recv.at[i], sibling))
        stage[mine, :] = fold[c]

    depth, width = e1.shape[1], w1.shape[2]
    cols = lambda n: pl.ds(pl.multiple_of(width * n, 128), width)
    strip = lambda n: pl.ds(pl.multiple_of(depth * n, 16), depth)
    half2, half2s = e2.shape[1], f2.shape[0]
    at2 = lambda core: pl.ds(pl.multiple_of(half2 * core, 16), half2)
    at2s = lambda core: pl.ds(pl.multiple_of(half2s * core, 16), half2s)
    local = [
        pltpu.make_async_copy(e1.at[:, :, cols(k)], w1.at[:, strip(gy), :], l_sem.at[0]),
        pltpu.make_async_copy(e2, w2.at[:, at2(c), :], l_sem.at[1]),
        pltpu.make_async_copy(f2, w2s.at[at2s(c), :], l_sem.at[2]),
    ]
    for copy in local:
        copy.start()
    plane = [o for o in others if o[0] == 0]

    def send_experts(steps):
        for i, o in enumerate(plane):
            if o[1] in steps:
                ty, tz, tx = spot(*o)
                go(remote(e1.at[:, :, cols(2 * tz + tx)], w1.at[:, strip(gy), :], a_send.at[i], a_recv.at[k], device(ty, tz, tx, c)))

    send_experts((0, 1))

    for i, (stage, block) in enumerate(((q_stage, q_block), (o_stage, o_block))):
        theirs = stage.at[pl.ds(pl.multiple_of(rows * (1 - c), 8), rows), :]
        remote(theirs, theirs, pre_send.at[i], pre_recv.at[i], sibling).wait_recv()
        block[...] = low(stage[...])
    gathers = []
    for i, (block, full, y_first) in enumerate(((q_block, q_full, False), (o_block, o_full, True))):
        slot = functools.partial(lambda full, n: full.at[c, pl.ds(pl.multiple_of(2 * rows * n, 16), 2 * rows), :], full)
        gathers.append(Gather(here, y_first, block, slot, g_send.at[i], g_recv.at[i], g_pair.at[i]))
        slot(me)[...] = block[...]
    gather_start(gathers)

    c_buf[number] = cond[number]
    for peer in peers:
        block = c_buf.at[2 * chip(*peer[:3]) + peer[3]]
        remote(block, block, c_send.at[0], c_recv.at[2 * chip(*peer[:3]) + peer[3]], sibling).wait_recv()
    for gz in range(4):
        for gy_ in range(2):
            group = [c_buf[2 * chip(gy_, gz, gx_) + core] for gx_ in (0, 1) for core in (0, 1)]
            conds[pl.ds(8 * (2 * gz + gy_), 8), :] = group[0] + group[1] + group[2] + group[3]
    lhs = low(conds[...])[:, :rows]
    for h in (0, 1):
        at = slice(h * part.shape[2], (h + 1) * part.shape[2])
        part[h] = nn(lhs, w_ada[:, at])
    go(remote(part.at[1 - c], sib, m_send.at[0], m_recv.at[0], sibling))

    gather_second(gathers, 0)
    remote(sib, sib, m_send.at[0], m_recv.at[0], sibling).wait_recv()
    for gz in range(4):
        at = slice(16 * gz, 16 * (gz + 1))
        z_part[gz] = part[c, at, :] + sib[at, :]
    for step in LINE:
        go(remote(z_part.at[(z + step) % 4], z_got.at[step - 1], m_send.at[step], m_recv.at[step], device(y, (z + step) % 4, x, c)))
    gather_line(gathers, 1)
    send_experts((3,))
    slim = w1s.shape[1]
    for n in range(16):
        block = wide_float(w_fc1[:, slim * n : slim * (n + 1)])
        f1[n] = low(jnp.concatenate([block, jnp.zeros((f1.shape[1] - rows, slim), jnp.float32)], axis=0))
    for i, o in enumerate(others):
        ty, tz, tx = spot(*o)
        go(remote(f1.at[chip(ty, tz, tx)], s_got.at[c, me], b_send.at[i], b_recv.at[me], device(ty, tz, tx, c)))
    s_got[c, me] = f1[me]
    gather_second(gathers, 1)
    gather_line(gathers, 3)
    send_experts((2,))
    total = wide_float(z_part[z])
    for step in LINE:
        remote(z_got.at[step - 1], z_got.at[step - 1], m_send.at[0], m_recv.at[step], sibling).wait_recv()
        total = total + wide_float(z_got[step - 1])
    xy_part[0] = total
    go(remote(xy_part.at[0], xy_got.at[0], m_send.at[4], m_recv.at[4], device(y, z, 1 - x, c)))
    gather_second(gathers, 3)
    remote(xy_got.at[0], xy_got.at[0], m_send.at[0], m_recv.at[4], sibling).wait_recv()
    xy_part[1] = xy_part[0] + xy_got[0]
    go(remote(xy_part.at[1], xy_got.at[1], m_send.at[5], m_recv.at[5], device(1 - y, z, x, c)))
    gather_line(gathers, 2)
    remote(xy_got.at[1], xy_got.at[1], m_send.at[0], m_recv.at[5], sibling).wait_recv()
    mod[c] = xy_part[1] + xy_got[1]
    go(remote(mod.at[c], mod.at[c], m_send.at[6], m_recv.at[6], sibling))
    gather_second(gathers, 2)
    twin = [
        remote(e2, w2.at[:, at2(c), :], d_send.at[0], d_recv.at[0], sibling),
        remote(f2, w2s.at[at2s(c), :], d_send.at[1], d_recv.at[1], sibling),
    ]
    for copy in twin:
        go(copy)
    remote(mod.at[1 - c], mod.at[1 - c], m_send.at[0], m_recv.at[6], sibling).wait_recv()

    item = item_mask(lengths, tokens.shape)
    residual = wide_float(tokens[...])
    normed, _ = norm(residual)
    attn_in[...] = low(normed * (1.0 + own_modulation(here, mod, item, 0, 1)) + own_modulation(here, mod, item, 0, 0))
    grad[...] = low(wide_float(cotangent[...]) * own_modulation(here, mod, item, 1, 2))
    for step in (0,) + LINE:
        gather_third(gathers, step)
    for gather in gathers:
        gather.finish()
    keep = [pltpu.make_async_copy(q_full, qkv_w, l_sem.at[4]), pltpu.make_async_copy(o_full, out_w, l_sem.at[5])]
    for copy in keep:
        copy.start()

    cut = q_full.shape[2]
    for h in (0, 1):
        qkv[:, h * cut : (h + 1) * cut] = low(nn(attn_in[...], q_full[h]))

    for copy in local:
        copy.wait()
    for i, o in enumerate([(0, 0, 0)] + [o for step in (0, 1, 3, 2) for o in plane if o[1] == step]):
        _, sz, sx = spot(*o)
        source = 2 * sz + sx
        block = w1.at[:, strip(2 * source + c), :]
        if i:
            remote(block, block, a_send.at[0], a_recv.at[source], sibling).wait_recv()
        go(remote(block, block, a_pair_send.at[i], a_pair.at[source], sibling))
    for o in others:
        n = chip(*spot(*o))
        remote(s_got.at[c, n], s_got.at[c, n], b_send.at[0], b_recv.at[n], sibling).wait_recv()
    go(remote(s_got.at[c], s_got.at[c], b_pair.at[0], b_pair.at[1], sibling))

    side = wide_float(item[:, :128])
    same = side == side.T
    left, sides = head_lanes()
    for pair in range(model // 128):
        q, key, value = [qkv[:, base + 128 * pair : base + 128 * (pair + 1)] for base in (0, model, 2 * model)]
        outs = []
        for j, side in enumerate(sides):
            scores = jnp.where(same, nt(q * side, key) * 0.125, -1e30)
            weight = jnp.exp(scores - jnp.max(scores, axis=-1, keepdims=True))
            prob = weight / jnp.sum(weight, axis=-1, keepdims=True)
            probs[2 * pair + j] = prob
            outs.append(nn(low(prob), value))
        attn_low[:, 128 * pair : 128 * (pair + 1)] = low(jnp.where(left, outs[0], outs[1]))
    cut = model // 2
    for h in (0, 1):
        attn_proj[:, h * cut : (h + 1) * cut] = nn(attn_low[...], o_full[h, :, :cut])
    middle[...] = residual + own_modulation(here, mod, item, 0, 2) * attn_proj[...]
    normed, _ = norm(middle[...])
    mixed[...] = low(normed * (1.0 + own_modulation(here, mod, item, 1, 1)) + own_modulation(here, mod, item, 1, 0))
    lane = lax.broadcasted_iota(jnp.int32, (1, 128), 1)
    logits = jnp.where(lane < 8, nn(mixed[...], o_full[0, :, cut:]), -1e30)
    weight = jnp.exp(logits - jnp.max(logits, axis=-1, keepdims=True))
    chance[...] = weight / jnp.sum(weight, axis=-1, keepdims=True)
    turned = jnp.where(choices(routes, square), chance[...], 0.0).T[:8]
    high = low(turned)
    gates[...] = jnp.concatenate([high, low(turned - wide_float(high))], axis=0)

    for copy in keep:
        copy.wait()
    for copy in started:
        copy.wait_send()
    for source in range(8):
        block = w1.at[:, strip(2 * source + 1 - c), :]
        remote(block, block, a_send.at[0], a_pair.at[source], sibling).wait_recv()
    remote(s_got.at[1 - c], s_got.at[1 - c], b_pair.at[0], b_pair.at[1], sibling).wait_recv()
    for n in range(32):
        s_rows[n * rows : (n + 1) * rows, :] = wide_float(s_got[n % 2, n // 2])[:rows]
    w1s[...] = low(s_rows[...])
    remote(w2.at[:, at2(1 - c), :], w2.at[:, at2(1 - c), :], d_send.at[0], d_recv.at[0], sibling).wait_recv()
    remote(w2s.at[at2s(1 - c), :], w2s.at[at2s(1 - c), :], d_send.at[1], d_recv.at[1], sibling).wait_recv()


def front(lengths, tokens, cotangent, routes, condition, w_ada, w_qkv, w_out, w_router, w_fc1, w_fc2, e_fc1, e_fc2):
    rows, model = w_out.shape
    toks = tokens.shape[0]
    y, z, x, c = place()
    cond = condition.astype(jnp.float32).reshape(-1, 32, rows).transpose(1, 0, 2)
    spot = jnp.arange(8) == (4 * x + 2 * c + jnp.arange(2))[:, None]
    cond = jnp.einsum("dir,is->dsr", cond, spot.astype(jnp.float32), precision=precise)
    cond = jnp.pad(cond, ((0, 0), (0, 0), (0, 128 - rows)))
    ff = w_fc1.shape[1]
    slim, wide = ff // 16, ff // 8
    experts = e_fc1.shape[0]
    bf, f32 = jnp.bfloat16, jnp.float32
    shape = jax.ShapeDtypeStruct
    q_half, o_half, a_half = w_qkv.shape[1] // 2, w_out.shape[1] // 2 + 128, w_ada.shape[1] // 2
    result = pl.pallas_call(
        front_kernel,
        out_shape=(
            shape((experts, model, wide), bf),
            shape((model, slim), bf),
            shape((experts, 2 * e_fc2.shape[1], model), bf),
            shape((2 * w_fc2.shape[0], model), bf),
            shape((2, model, q_half), bf),
            shape((2, model, o_half), bf),
            shape((64, 128), f32),
            shape((2, 16, a_half), f32),
            shape((toks, model), bf),
            shape((toks, model), bf),
            shape((16, toks), bf),
            shape((toks, model), bf),
            shape((toks, 3 * model), bf),
            shape((HEADS, toks, toks), f32),
            shape((toks, model), bf),
            shape((toks, model), f32),
            shape((toks, model), f32),
            shape((toks, 128), f32),
        ),
        in_specs=[pl.BlockSpec(memory_space=pltpu.SMEM)]
        + [pl.BlockSpec(memory_space=VMEM)] * 9
        + [pl.BlockSpec(memory_space=ANY)] * 3,
        out_specs=[pl.BlockSpec(memory_space=ANY), pl.BlockSpec(memory_space=VMEM)]
        + [pl.BlockSpec(memory_space=ANY)] * 4
        + [pl.BlockSpec(memory_space=VMEM)] * 12,
        scratch_shapes=[
            VMEM((128, 128), f32), VMEM((16, 32, slim), bf), VMEM((2, 16, 32, slim), bf), VMEM((model, slim), f32),
            VMEM((2, model, q_half), bf), VMEM((2, model, o_half), bf),
            VMEM((2, rows, q_half), f32), VMEM((2, rows, o_half), f32), VMEM((2 * rows, q_half), f32), VMEM((2 * rows, o_half), f32),
            VMEM((2 * rows, q_half), bf), VMEM((2 * rows, o_half), bf),
            VMEM((32, 8, 128), f32), VMEM((2, 64, a_half), f32), VMEM((64, a_half), f32),
            VMEM((4, 16, a_half), f32), VMEM((3, 16, a_half), f32), VMEM((2, 16, a_half), f32), VMEM((2, 16, a_half), f32),
            DMA((2,)), DMA((2,)), DMA((2, 31)), DMA((2, 16)), DMA((2, 16)), DMA((7,)), DMA((8,)), DMA((8,)), DMA((8,)),
            DMA((15,)), DMA((16,)), DMA((2,)), DMA((6,)), DMA((2,)), DMA((2,)), DMA((31,)), DMA((32,)), DMA((7,)), DMA((7,)),
        ],
        compiler_params=pltpu.CompilerParams(collective_id=1, has_side_effects=True, vmem_limit_bytes=62 << 20),
        name="front",
    )(lengths, tokens, cotangent, routes.T, cond, w_ada, w_qkv, w_out, w_router.T, w_fc1, e_fc1, e_fc2, w_fc2)
    return result


def gelu_both(h):
    root = math.sqrt(2.0 / math.pi)
    square = h * h
    t = jnp.tanh(h * (root + (root * 0.044715) * square))
    half = 0.5 * (1.0 + t)
    slope = half + (0.5 * h) * (1.0 - t * t) * (root + (3.0 * root * 0.044715) * square)
    return h * half, slope


def ffn_chunk(xt, gt, w1, w2, gate, row):
    a, d = gelu_both(nn(xt, w1))
    gi = nt(gt, w2)
    product = None
    if gate is not None:
        product = nt(row, (a * gi).astype(jnp.bfloat16))
        a, d = a * gate, d * gate
    a = a.astype(jnp.bfloat16)
    p = (gi * d).astype(jnp.bfloat16)
    return a, p, nn(a, w2), nt(p, w1), product


def ffn_shared(slots, X, G, w1s, w2s, act_s, pre_s, sums, sums_back):
    toks = X.shape[1]
    xt = jnp.concatenate([X[n] for n in slots], axis=0)
    gt = jnp.concatenate([G[n] for n in slots], axis=0)
    a, p, total, total_back, _ = ffn_chunk(xt, gt, w1s[...], w2s[...], None, None)
    for i, n in enumerate(slots):
        act_s[n] = a[i * toks : (i + 1) * toks]
        pre_s[n] = p[i * toks : (i + 1) * toks]
    sums[...] = total
    sums_back[...] = total_back


def ffn_experts(low, high, slots, X, G, gates, w1, w2, act, pre, sums, sums_back, gc):
    experts, toks, wide = w1.shape[0], X.shape[1], w1.shape[2]
    first = lax.axis_index("gx") * experts
    xt = jnp.concatenate([X[n] for n in slots], axis=0)
    gt = jnp.concatenate([G[n] for n in slots], axis=0)

    def expert(e, product):
        kind = lax.broadcasted_iota(jnp.int32, (16, 128), 0)
        spread = ((kind == first + e) | (kind == first + e + 8)).astype(jnp.bfloat16)
        gate = jnp.concatenate([tn(gates[n], spread) for n in slots], axis=0)
        gate = jnp.concatenate([gate] * (wide // 128), axis=1)
        row = (lax.broadcasted_iota(jnp.int32, (8, wide), 0) == first + e).astype(jnp.bfloat16)
        a, p, total, total_back, more = ffn_chunk(xt, gt, w1[e], w2[e], gate, row)
        for i, n in enumerate(slots):
            act[e, n] = a[i * toks : (i + 1) * toks]
            pre[e, n] = p[i * toks : (i + 1) * toks]
        sums[...] += total
        sums_back[...] += total_back
        return product + more

    product = lax.fori_loop(low, high, expert, jnp.zeros((8, len(slots) * toks), jnp.float32))
    for i, n in enumerate(slots):
        part = product[:, i * toks : (i + 1) * toks]
        gc[n] = part if low == 0 else gc[n] + part


def block_kernel(
    mixed, grad, gates, w1_in, w1s_in, w2_in, w2s_in,
    sum_branch, sum_back, sum_gc, own1, own1s, own2, own2s,
    X, G, gt, w1, w1s, w2, w2s, act, pre, act_s, pre_s, tile_sum, tile_back,
    p_branch, p_back, p_gc, r_branch, r_back, r_gc, d1, d1s, d2, d2s, from1, from1s, from2, from2s,
    l_sem, g_send, g_recv, send, recv, t_send, t_recv,
):
    here = y, z, x, c = place()
    me = chip(y, z, x)
    spot = lambda dy, dz, dx: (1 - y if dy else y, (z + dz) % 4, 1 - x if dx else x)
    sibling = device(y, z, x, 1 - c)
    experts = w1.shape[0]
    meet(cross_partners(here) + [sibling])

    gathers, local = [], []
    for i, (block, full, y_first) in enumerate(((mixed, X, True), (grad, G, False), (gates, gt, True))):
        slot = functools.partial(lambda full, n: full.at[n], full)
        gathers.append(Gather(here, y_first, block, slot, g_send.at[i], g_recv.at[i]))
        local.append(pltpu.make_async_copy(block, slot(me), l_sem.at[i]))
    gather_start(gathers)
    for i, (source, target) in enumerate(((w1_in, w1), (w1s_in, w1s), (w2_in, w2), (w2s_in, w2s))):
        local.append(pltpu.make_async_copy(source, target, l_sem.at[3 + i]))
    for copy in local:
        copy.start()

    def tile(step, part):
        slots = [chip(*spot(dy, step, dx)) for dy in (0, 1) for dx in (0, 1)]
        if part == 0:
            ffn_shared(slots, X, G, w1s, w2s, act_s, pre_s, tile_sum, tile_back)
        low, high = (0, experts // 2) if part == 0 else (experts // 2, experts)
        ffn_experts(low, high, slots, X, G, gt, w1, w2, act, pre, tile_sum, tile_back, p_gc)
        if part == 1:
            toks = X.shape[1]
            for i, n in enumerate(slots):
                at = slice(i * toks, (i + 1) * toks)
                p_branch[n] = tile_sum[at, :].astype(jnp.bfloat16)
                p_back[n] = tile_back[at, :].astype(jnp.bfloat16)

    scatters = []
    for i, (part, got, y_first) in enumerate(((p_branch, r_branch, False), (p_back, r_back, True), (p_gc, r_gc, False))):
        take = functools.partial(lambda ref, n: ref.at[n], part)
        land = functools.partial(lambda ref, n: ref.at[n], got)
        scatters.append(Scatter(here, y_first, take, land, send.at[i], recv.at[i]))

    def back_first(step):
        for scatter in scatters:
            scatter.first(step)

    gather_second(gathers, 0)
    gather_line(gathers, 1)
    gather_second(gathers, 1)
    gather_third(gathers, 0)
    for copy in local:
        copy.wait()
    tile(0, 0)
    gather_line(gathers, 3)
    tile(0, 1)
    gather_third(gathers, 1)
    tile(1, 0)
    gather_second(gathers, 3)
    tile(1, 1)
    gather_line(gathers, 2)
    gather_third(gathers, 3)
    tile(3, 0)
    gather_second(gathers, 2)
    back_first(1)
    tile(3, 1)
    back_first(3)
    gather_third(gathers, 2)
    tile(2, 0)
    tile(2, 1)

    def back_one(step):
        for scatter in scatters:
            scatter.one(1, step)
        for scatter in scatters:
            scatter.one(0, step)

    def back_two(step):
        for scatter in scatters:
            scatter.two(step)

    flat = lambda value: value.reshape(value.shape[0] * value.shape[1], value.shape[2])
    twins = [None] * (2 * experts)

    def weight(e):
        d1[e] = tn(flat(X[...]), flat(pre[e])).astype(jnp.bfloat16).reshape(d1.shape[1:])
        d2[e] = tn(flat(act[e]), flat(G[...])).astype(jnp.bfloat16).reshape(d2.shape[1:])
        for i, (part, got) in enumerate(((d1.at[e, :, 1 - c], from1.at[e]), (d2.at[e, 1 - c], from2.at[e]))):
            twins[2 * e + i] = remote(part, got, t_send.at[2 * e + i], t_recv.at[2 * e + i], sibling)
            twins[2 * e + i].start()

    def home(e):
        twins[2 * e].wait()
        own1[e] = (d1[e, :, c].astype(jnp.float32) + from1[e].astype(jnp.float32)).astype(jnp.bfloat16)
        twins[2 * e + 1].wait()
        own2[e] = d2[e, c].astype(jnp.float32) + from2[e].astype(jnp.float32)

    back_one(1)
    back_first(2)
    back_two(1)
    weight(0)
    back_one(3)
    back_two(3)
    home(0)
    weight(1)
    back_one(2)
    back_first(0)
    back_two(2)
    home(1)
    weight(2)
    home(2)
    weight(3)
    d1s[...] = tn(flat(X[...]), flat(pre_s[...])).reshape(d1s.shape)
    d2s[...] = tn(flat(act_s[...]), flat(G[...])).astype(jnp.bfloat16).reshape(d2s.shape)
    twin1s = remote(d1s.at[:, 1 - c], from1s, t_send.at[2 * experts], t_recv.at[2 * experts], sibling)
    twin2s = remote(d2s.at[1 - c], from2s, t_send.at[2 * experts + 1], t_recv.at[2 * experts + 1], sibling)
    twin1s.start()
    twin2s.start()
    home(3)
    back_one(0)
    twin1s.wait()
    own1s[...] = d1s[:, c] + from1s[...]
    twin2s.wait()
    own2s[...] = d2s[c].astype(jnp.float32) + from2s[...].astype(jnp.float32)
    back_two(0)
    sum_branch[...] = scatters[0].total()
    sum_back[...] = scatters[1].total()
    sum_gc[...] = scatters[2].total()
    for gather in gathers:
        gather.finish()
    for scatter in scatters:
        scatter.finish()


def block(mixed, grad, gates, w1, w1s, w2, w2s):
    bf, f32 = jnp.bfloat16, jnp.float32
    toks, model = mixed.shape
    experts, _, wide = w1.shape
    slim = w1s.shape[1]
    rows = model // 32
    shape = jax.ShapeDtypeStruct
    blocks = lambda *dims: VMEM((16, toks) + dims, bf)
    return pl.pallas_call(
        block_kernel,
        out_shape=[
            shape((toks, model), f32),
            shape((toks, model), f32),
            shape((8, 128), f32),
            shape((experts, 8, 2 * rows, wide), bf),
            shape((16, rows, slim), f32),
            shape((experts, wide // 2, model), f32),
            shape((slim // 2, model), f32),
        ],
        in_specs=[pl.BlockSpec(memory_space=VMEM)] * 3 + [pl.BlockSpec(memory_space=ANY)] * 4,
        out_specs=[pl.BlockSpec(memory_space=VMEM)] * 7,
        scratch_shapes=[
            blocks(model), blocks(model), VMEM((16, 16, 128), bf),
            VMEM(w1.shape, bf), VMEM(w1s.shape, bf), VMEM(w2.shape, bf), VMEM(w2s.shape, bf),
            VMEM((experts, 16, toks, wide), bf), VMEM((experts, 16, toks, wide), bf), blocks(slim), blocks(slim),
            VMEM((4 * toks, model), f32), VMEM((4 * toks, model), f32),
            blocks(model), blocks(model), VMEM((16, 8, 128), f32),
            VMEM((15, toks, model), bf), VMEM((15, toks, model), bf), VMEM((15, 8, 128), f32),
            VMEM((experts, 8, 2, 2 * rows, wide), bf), VMEM((16, 2, rows, slim), f32),
            VMEM((experts, 2, wide // 2, model), bf), VMEM((2, slim // 2, model), bf),
            VMEM((experts, 8, 2 * rows, wide), bf), VMEM((16, rows, slim), f32),
            VMEM((experts, wide // 2, model), bf), VMEM((slim // 2, model), bf),
            DMA((7,)), DMA((3, 15)), DMA((3, 16)), DMA((3, 15)), DMA((3, 15)), DMA((2 * experts + 2,)), DMA((2 * experts + 2,)),
        ],
        compiler_params=pltpu.CompilerParams(collective_id=2, has_side_effects=True, vmem_limit_bytes=62 << 20),
        name="block",
    )(mixed, grad, gates, w1, w1s, w2, w2s)


def rear_kernel(
    lengths, sum_branch, sum_back, sum_gc, tokens, cotangent, routes, mod, conds, mixed, attn_in, qkv, probs, attn_low, attn_proj, middle,
    chance, qkv_in, out_in, part1, part1s,
    output, d_tokens, d_ada, d_qkv, d_out, d_router, own1, own1s,
    square, q_w, o_w, grad_attn, grad_qkv, grad_mid, o_mine, o_got, q_mine, q_got, part_o, part_a, part_b,
    got_o, got_a, got_b, fin, mod_tile, all_mod,
    l_sem, s_send, s_recv, send, recv, g_send, g_recv, g_pair, f_send, f_recv, a_send, a_recv, b_send, b_recv,
):
    here = y, z, x, c = place()
    me, k = chip(y, z, x), 2 * z + x
    sibling = device(y, z, x, 1 - c)
    others = [(dy, dz, dx) for dy in (0, 1) for dz in (0, 1, 2, 3) for dx in (0, 1) if (dy, dz, dx) != (0, 0, 0)]
    plane = [o for o in others if o[0] == 0]
    spot = lambda dy, dz, dx: (1 - y if dy else y, (z + dz) % 4, 1 - x if dx else x)
    local = [pltpu.make_async_copy(qkv_in, q_w, l_sem.at[0]), pltpu.make_async_copy(out_in, o_w, l_sem.at[1])]
    for copy in local:
        copy.start()
    meet([device(*spot(*o), c) for o in others] + [sibling])
    started = []

    def go(copy):
        copy.start()
        started.append(copy)

    wide = part1.shape[3]
    columns = lambda n: own1.at[:, :, pl.ds(pl.multiple_of(wide * n, 128), wide)]
    home = [pltpu.make_async_copy(part1.at[:, k], columns(k), l_sem.at[2]), pltpu.make_async_copy(part1s.at[me], own1s.at[me], l_sem.at[3])]
    for copy in home:
        copy.start()
    for i, o in enumerate(plane):
        ty, tz, tx = spot(*o)
        go(remote(part1.at[:, 2 * tz + tx], columns(k), a_send.at[i], a_recv.at[k], device(ty, tz, tx, c)))
    for i, o in enumerate(others):
        go(remote(part1s.at[chip(*spot(*o))], own1s.at[me], b_send.at[i], b_recv.at[me], device(*spot(*o), c)))

    item = item_mask(lengths, tokens.shape)
    first = ~item
    model = item.shape[1]
    cut = model // 2
    modulation = functools.partial(own_modulation, here, mod, item)
    rows16 = {}

    def per_item(part, value):
        for i, mask in enumerate((first, ~first)):
            rows16[2 * part + i] = jnp.sum(jnp.where(mask, value, 0.0), axis=0, keepdims=True)

    out_grad = wide_float(cotangent[...])
    branch = sum_branch[...]
    output[...] = low(middle[...] + modulation(1, 2) * branch)
    per_item(5, out_grad * branch)
    chosen = choices(routes, square)
    turned = jnp.concatenate([sum_gc[...], jnp.zeros((120, 128), jnp.float32)], axis=0).T
    grad_chance = jnp.where(chosen, turned, 0.0)
    share = chance[...]
    grad_logits = low(share * (grad_chance - jnp.sum(grad_chance * share, axis=-1, keepdims=True)))
    term_router = tn(mixed[...], grad_logits)
    for copy in local:
        copy.wait()
    grad_mixed = sum_back[...] + nt(grad_logits, o_w[0, :, cut:])
    normed, scale = norm(middle[...])
    per_item(3, grad_mixed)
    per_item(4, grad_mixed * normed)
    grad_mid[...] = out_grad + norm_back(grad_mixed * (1.0 + modulation(1, 1)), normed, scale)
    per_item(2, grad_mid[...] * attn_proj[...])
    grad_proj = low(grad_mid[...] * modulation(0, 2))
    for h in (0, 1):
        term = jnp.concatenate([tn(attn_low[...], grad_proj[:, h * cut : (h + 1) * cut]), term_router], axis=1)
        o_mine[h] = low(term)
    swap_o = remote(o_mine.at[1 - c], o_got, s_send.at[0], s_recv.at[0], sibling)
    swap_o.start()
    grad_attn[...] = low(nt(grad_proj[:, :cut], o_w[0, :, :cut]) + nt(grad_proj[:, cut:], o_w[1, :, :cut]))

    rows = o_got.shape[0] // 16
    scatters = []
    for i, (part, got, y_first) in enumerate(((part_o, got_o, False), (part_a, got_a, True), (part_b, got_b, False))):
        take = functools.partial(lambda ref, n: ref.at[n], part)
        land = functools.partial(lambda ref, n: ref.at[n], got)
        scatters.append(Scatter(here, y_first, take, land, send.at[i], recv.at[i]))

    def out_stage(stage):
        tool = scatters[0]
        if stage == 0:
            swap_o.wait()
            for n in range(16):
                at = slice(n * rows, (n + 1) * rows)
                part_o[n] = low(wide_float(o_mine[c, at, :]) + wide_float(o_got[at, :]))
            for step in (2, 1, 3, 0):
                tool.first(step)
        else:
            for step in ((2,), (1, 3), (0,))[stage - 1]:
                tool.one(1, step)
                tool.one(0, step)
        if stage > 1:
            for step in ((2,), (1, 3))[stage - 2]:
                tool.two(step)

    left, sides = head_lanes()
    for pair in range(model // 128):
        at = slice(128 * pair, 128 * (pair + 1))
        q, key, value = [qkv[:, base + 128 * pair : base + 128 * (pair + 1)] for base in (0, model, 2 * model)]
        ga = grad_attn[:, at]
        outs = []
        for j, side in enumerate(sides):
            prob = probs[2 * pair + j]
            grad_probs = nt(ga * side, value)
            grad_scores = low(prob * (grad_probs - jnp.sum(grad_probs * prob, axis=-1, keepdims=True)))
            outs.append((nn(grad_scores, key) * 0.125, tn(grad_scores, q) * 0.125, tn(low(prob), ga)))
        for base, one, two in zip((0, model, 2 * model), *outs):
            grad_qkv[:, base + 128 * pair : base + 128 * (pair + 1)] = low(jnp.where(left, one, two))
        if pair in (1, 3, 5):
            out_stage(pair // 2)

    third = q_w.shape[2]
    for h in (0, 1):
        q_mine[h] = low(tn(attn_in[...], grad_qkv[:, h * third : (h + 1) * third]))
    swap_q = remote(q_mine.at[1 - c], q_got, s_send.at[1], s_recv.at[1], sibling)
    swap_q.start()
    out_stage(3)
    grad_in = nt(grad_qkv[:, :third], q_w[0]) + nt(grad_qkv[:, third:], q_w[1])
    normed, scale = norm(wide_float(tokens[...]))
    per_item(0, grad_in)
    per_item(1, grad_in * normed)
    d_tokens[...] = grad_mid[...] + norm_back(grad_in * (1.0 + modulation(0, 1)), normed, scale)
    rows16[12] = jnp.zeros((4, model), jnp.float32)
    mod_tile[...] = low(jnp.concatenate([rows16[i] for i in range(13)], axis=0))

    slot = lambda n: all_mod.at[n, c]
    spread = Gather(here, True, mod_tile, slot, g_send, g_recv, g_pair)
    all_mod[me, c] = mod_tile[...]
    gather_start([spread])
    swap_q.wait()
    edge = part_a.shape[2]
    for n in range(16):
        at = slice(n * rows, (n + 1) * rows)
        total = low(wide_float(q_mine[c, at, :]) + wide_float(q_got[at, :]))
        part_a[n] = total[:, :edge]
        part_b[n] = total[:, edge:]

    def turn(at):
        if at == 0:
            scatters[0].two(0)
            spread.second(0)
            for step in LINE:
                gather_line([spread], step)
        elif at == 1:
            for step in LINE:
                spread.second(step)
        elif at == 2:
            for step in (0,) + LINE:
                spread.third(step)
            spread.finish()

    scatter_all(scatters[1:], turn)
    fin[c] = jnp.concatenate([scatters[1].total(), scatters[2].total(), scatters[0].total()], axis=1)
    half = rows // 2
    mine = pl.ds(pl.multiple_of(half * c, 8), half)
    theirs = pl.ds(pl.multiple_of(half * (1 - c), 8), half)
    swap = remote(fin.at[c, theirs, :], fin.at[c, theirs, :], f_send, f_recv, sibling)
    swap.start()

    flat = all_mod[...].reshape(32 * 16, model)
    row = lax.broadcasted_iota(jnp.int32, (64, 512), 1)
    spot_of = row // 16
    place_of = 16 * ((spot_of // 4) % 4) + 8 * (spot_of // 16) + 4 * ((spot_of // 2) % 2) + 2 * (spot_of % 2) + row % 2
    meets = lax.broadcasted_iota(jnp.int32, (64, 512), 0) == place_of
    columns_in = low(conds[...])
    for part in range(6):
        pick = low(wide_float(meets & ((row % 16) // 2 == part)))
        lhs = low(tn(columns_in, pick))
        d_ada[:, part * model : (part + 1) * model] = nn(lhs, flat)[: d_ada.shape[0]]

    for i, o in enumerate(plane):
        n = 2 * spot(*o)[1] + spot(*o)[2]
        remote(columns(n), columns(n), a_send.at[i], a_recv.at[n], sibling).wait_recv()
    for copy in home:
        copy.wait()
    for i, o in enumerate(others):
        n = chip(*spot(*o))
        remote(own1s.at[n], own1s.at[n], b_send.at[i], b_recv.at[n], sibling).wait_recv()
    for scatter in scatters:
        scatter.finish()
    for copy in started:
        copy.wait_send()
    swap.wait_send()
    remote(fin.at[1 - c, mine, :], fin.at[1 - c, mine, :], f_send, f_recv, sibling).wait_recv()
    for h in (0, 1):
        d_qkv[:, h * third : (h + 1) * third] = fin[h, mine, :third]
        d_out[:, h * cut : (h + 1) * cut] = fin[h, mine, third : third + cut]
    d_router[0:half, :] = fin[0, mine, third + cut :]
    d_router[half:, :] = jnp.zeros((128 - half, 128), jnp.float32)


def rear(lengths, sums, tokens, cotangent, routes, saved, qkv_w, out_w, part1, part1s):
    bf, f32 = jnp.bfloat16, jnp.float32
    toks, model = tokens.shape
    rows = model // 16
    experts, _, depth, wide = part1.shape
    q_half, o_half = qkv_w.shape[2], out_w.shape[2]
    a_half = model
    shape = jax.ShapeDtypeStruct
    return pl.pallas_call(
        rear_kernel,
        out_shape=[
            shape((toks, model), bf),
            shape((toks, model), f32),
            shape((rows // 2, 6 * model), f32),
            shape((rows // 2, 2 * q_half), f32),
            shape((rows // 2, model), f32),
            shape((128, 128), f32),
            shape((experts, depth, 8 * wide), bf),
            shape(part1s.shape, f32),
        ],
        in_specs=[pl.BlockSpec(memory_space=pltpu.SMEM)]
        + [pl.BlockSpec(memory_space=VMEM)] * 16
        + [pl.BlockSpec(memory_space=ANY)] * 4,
        out_specs=[pl.BlockSpec(memory_space=VMEM)] * 6 + [pl.BlockSpec(memory_space=ANY)] * 2,
        scratch_shapes=[
            VMEM((128, 128), f32), VMEM(qkv_w.shape, bf), VMEM(out_w.shape, bf),
            VMEM((toks, model), bf), VMEM((toks, 3 * model), bf), VMEM((toks, model), f32),
            VMEM((2, model, o_half), bf), VMEM((model, o_half), bf),
            VMEM((2, model, q_half), bf), VMEM((model, q_half), bf),
            VMEM((16, rows, o_half), bf), VMEM((16, rows, a_half), bf), VMEM((16, rows, q_half - a_half), bf),
            VMEM((15, rows, o_half), bf), VMEM((15, rows, a_half), bf), VMEM((15, rows, q_half - a_half), bf),
            VMEM((2, rows, q_half + o_half), f32), VMEM((16, model), bf), VMEM((16, 2, 16, model), bf),
            DMA((4,)), DMA((2,)), DMA((2,)), DMA((3, 15)), DMA((3, 15)), DMA((31,)), DMA((16,)), DMA((16,)), DMA, DMA,
            DMA((7,)), DMA((8,)), DMA((15,)), DMA((16,)),
        ],
        compiler_params=pltpu.CompilerParams(collective_id=3, has_side_effects=True, vmem_limit_bytes=62 << 20),
        name="rear",
    )(lengths, *sums, tokens, cotangent, routes.T, *saved, qkv_w, out_w, part1, part1s)


def finish_kernel(*refs):
    count = (len(refs) - 4) // 3
    inputs, outputs, staged = refs[:count], refs[count : 2 * count], refs[2 * count : 3 * count]
    e1, fc1, sem_in, sem = refs[3 * count :]
    loads = [pltpu.make_async_copy(a, b, sem_in.at[i]) for i, (a, b) in enumerate(zip(inputs, staged))]
    stores = []

    def store(source, target):
        stores.append(pltpu.make_async_copy(source, target, sem.at[len(stores)]))
        stores[-1].start()

    for copy in loads:
        copy.start()
    low_e1, slices, router = staged[:3]
    loads[0].wait()
    for e in range(low_e1.shape[0]):
        e1[e] = wide_float(low_e1[e])
        store(e1.at[e], outputs[0].at[e])
    for load, source, target in zip(loads[3:], staged[3:], outputs[3:]):
        load.wait()
        store(source, target)
    loads[1].wait()
    loads[2].wait()
    slim = slices.shape[2]
    for n in range(slices.shape[0] // 2):
        fc1[:, 2 * n * slim : 2 * (n + 1) * slim] = jnp.concatenate([slices[2 * n], slices[2 * n + 1]], axis=1)
    store(fc1, outputs[1])
    outputs[2][...] = router[...].T[: outputs[2].shape[0]]
    for copy in stores:
        copy.wait()


def finish(own1, own1s, d_router, *others):
    f32 = jnp.float32
    rows = own1s.shape[1]
    wide = (rows, own1s.shape[0] * own1s.shape[2])
    shape = jax.ShapeDtypeStruct
    result = pl.pallas_call(
        finish_kernel,
        out_shape=[shape(own1.shape, f32), shape(wide, f32), shape((8, 128), f32)] + [shape(a.shape, a.dtype) for a in others],
        in_specs=[pl.BlockSpec(memory_space=ANY)] * (3 + len(others)),
        out_specs=[pl.BlockSpec(memory_space=ANY)] * 2
        + [pl.BlockSpec(memory_space=VMEM)]
        + [pl.BlockSpec(memory_space=ANY)] * len(others),
        scratch_shapes=[VMEM(a.shape, a.dtype) for a in (own1, own1s, d_router, *others)]
        + [VMEM(own1.shape, f32), VMEM(wide, f32), DMA((3 + len(others),)), DMA((8 + len(others),))],
        compiler_params=pltpu.CompilerParams(vmem_limit_bytes=62 << 20),
        name="finish",
    )(own1, own1s, d_router, *others)
    return result[0], result[1], result[2][:, :rows].T, *result[3:]


def layer_norm(values):
    average = jnp.mean(values, axis=-1, keepdims=True)
    centred = values - average
    return centred * lax.rsqrt(jnp.mean(centred * centred, axis=-1, keepdims=True) + layer_epsilon)


def modulate(values, shift_by, scale_by):
    return layer_norm(values) * (1.0 + scale_by) + shift_by


def sinusoid(timesteps, model_width):
    half_width = model_width // 2
    frequency = jnp.exp(-math.log(10000.0) * jnp.arange(half_width, dtype=jnp.float32) / half_width)
    angles = timesteps.astype(jnp.float32)[:, None] * frequency[None, :]
    return jnp.concatenate([jnp.cos(angles), jnp.sin(angles)], axis=1)


def membership(lengths, tok_count):
    bounds = jnp.cumsum(lengths)[:-1]
    position = jnp.arange(tok_count, dtype=jnp.int32)
    item_of = jnp.sum((position[:, None] >= bounds[None, :]).astype(jnp.int32), axis=1)
    item_ids = jnp.arange(lengths.shape[0], dtype=jnp.int32)
    return ((item_of[:, None] == item_ids[None, :]).astype(jnp.float32), item_of)


def slot_index(routes, expert_count, capacity):
    flat_routes = routes.reshape(-1)
    expert_hot = (
        flat_routes[:, None] == jnp.arange(expert_count, dtype=jnp.int32)[None, :]
    ).astype(jnp.int32)
    before = jnp.cumsum(expert_hot, axis=0) - expert_hot
    rank_in = jnp.sum(before * expert_hot, axis=1)
    return (flat_routes * capacity + rank_in).reshape(routes.shape)


def dot_float(left_side, right_side):
    return jnp.dot(left_side, right_side, preferred_element_type=jnp.float32)


def dot_rows(left_side, right_side):
    return jnp.einsum("td,tf->df", left_side, right_side, preferred_element_type=jnp.float32)


def dot_cols(left_side, right_side):
    return jnp.einsum("tf,df->td", left_side, right_side, preferred_element_type=jnp.float32)


def dot_halves(left_side, halves):
    return jnp.concatenate([dot_float(left_side, halves[0]), dot_float(left_side, halves[1])], axis=1)


def by_slices(
    tokens, timesteps, lengths, routes, cotangent, w_ada, w_qkv, w_out, w_fc1, w_fc2, w_router, e_fc1, e_fc2
):
    model_width = tokens.shape[1]
    condition = jax.nn.silu(sinusoid(timesteps, model_width)).astype(jnp.bfloat16)
    (w1, w1s, w2, w2s, qkv_w, out_w, conds, mod, mixed, grad, gates, attn_in, qkv, probs, attn_low, attn_proj, middle,
     chance) = front(
        lengths, tokens, cotangent, routes, condition, w_ada, w_qkv, w_out, w_router, w_fc1, w_fc2, e_fc1, e_fc2
    )
    *sums, part1, part1s, d_e2, d_fc2 = block(mixed, grad, gates, w1, w1s, w2, w2s)
    saved = (mod, conds, mixed, attn_in, qkv, probs, attn_low, attn_proj, middle, chance)
    output, d_tokens, d_ada, d_qkv, d_out, d_router, own1, own1s = rear(
        lengths, sums, tokens, cotangent, routes, saved, qkv_w, out_w, part1, part1s
    )
    d_e1, d_fc1, d_router, output, d_tokens, d_ada, d_qkv, d_out, d_fc2, d_e2 = finish(
        own1, own1s, d_router, output, d_tokens, d_ada, d_qkv, d_out, d_fc2, d_e2
    )
    return (output, d_tokens, d_ada, d_qkv, d_out, d_fc1, d_fc2, d_router, d_e1, d_e2)


def by_weights(
    tokens,
    timesteps,
    lengths,
    routes,
    cotangent,
    w_ada,
    w_qkv,
    w_out,
    w_fc1,
    w_fc2,
    w_router,
    e_fc1,
    e_fc2,
):
    tok_count, model_width = tokens.shape
    head_count = HEADS
    head_size = model_width // head_count
    expert_count = w_router.shape[1]
    capacity = CAP
    score_scale = head_size ** (-0.5)
    residual = tokens.astype(jnp.float32)
    member, item_of = membership(lengths[0], tok_count)
    ada_full, qkv_full, out_full = (
        lax.all_gather(w_ada, ("gx", "gy"), axis=0, tiled=True),
        lax.all_gather(w_qkv, ("gx", "gy"), axis=0, tiled=True),
        lax.all_gather(w_out, ("gx", "gy"), axis=0, tiled=True),
    )
    condition = jax.nn.silu(sinusoid(timesteps, model_width)).astype(jnp.bfloat16)
    modulation = dot_float(condition, ada_full)
    token_mod = jnp.dot(member, modulation, precision=precise)
    shift_attn, scale_attn, gate_attn, shift_mlp, scale_mlp, gate_mlp = jnp.split(
        token_mod, 6, axis=1
    )
    attn_in = modulate(residual, shift_attn, scale_attn).astype(jnp.bfloat16)
    qkv_low = dot_float(attn_in, qkv_full).astype(jnp.bfloat16)
    queries, key_rows, value_rows = [
        portion.reshape(tok_count, head_count, head_size)
        for portion in jnp.split(qkv_low, 3, axis=1)
    ]
    same_item = item_of[:, None] == item_of[None, :]
    scores = (
        jnp.einsum("qhd,khd->hqk", queries, key_rows, preferred_element_type=jnp.float32)
        * score_scale
    )
    scores = jnp.where(same_item[None], scores, -1e30)
    attn_probs = jax.nn.softmax(scores, axis=-1)
    probs_low = attn_probs.astype(jnp.bfloat16)
    attn_low = jnp.einsum("hqk,khd->qhd", probs_low, value_rows, preferred_element_type=jnp.float32)
    attn_low = attn_low.reshape(tok_count, model_width).astype(jnp.bfloat16)
    attn_proj = dot_float(attn_low, out_full)
    middle = residual + gate_attn * attn_proj
    mixed_in = modulate(middle, shift_mlp, scale_mlp).astype(jnp.bfloat16)
    fc1_full, fc2_full, router_full = (
        lax.all_gather(w_fc1, ("gx", "gy"), axis=0, tiled=True),
        lax.all_gather(w_fc2, ("gx", "gy"), axis=0, tiled=True),
        lax.all_gather(w_router, ("gx", "gy"), axis=0, tiled=True),
    )
    hidden_pre = dot_float(mixed_in, fc1_full)
    hidden = jax.nn.gelu(hidden_pre).astype(jnp.bfloat16)
    shared = dot_float(hidden, fc2_full)
    chance = jax.nn.softmax(dot_float(mixed_in, router_full), axis=-1)
    expert_ids = jnp.arange(expert_count, dtype=jnp.int32)
    chosen = (routes[:, :, None] == expert_ids[None, None, :]).astype(jnp.float32)
    gate_values = jnp.sum(chosen * chance[:, None, :], axis=2)
    slot_of = slot_index(routes, expert_count, capacity)
    slot_ids = jnp.arange(expert_count * capacity, dtype=jnp.int32)
    selector = (slot_of[:, :, None] == slot_ids[None, None, :]).astype(jnp.bfloat16)
    slot_rows = jnp.einsum("tks,td->sd", selector, mixed_in, preferred_element_type=jnp.float32)
    slot_rows = slot_rows.astype(jnp.bfloat16).reshape(expert_count, capacity, model_width)
    owned_rows = lax.all_to_all(slot_rows, "gx", split_axis=0, concat_axis=1, tiled=True)
    expert_in, expert_back = (
        lax.all_gather(e_fc1, "gy", axis=1, tiled=True),
        lax.all_gather(e_fc2, "gy", axis=1, tiled=True),
    )
    inner_pre = jnp.einsum(
        "ecd,edf->ecf", owned_rows, expert_in, preferred_element_type=jnp.float32
    )
    inner_act = jax.nn.gelu(inner_pre).astype(jnp.bfloat16)
    result = jnp.einsum(
        "ecf,efd->ecd", inner_act, expert_back, preferred_element_type=jnp.float32
    ).astype(jnp.bfloat16)
    returned = lax.all_to_all(result, "gx", split_axis=1, concat_axis=0, tiled=True).reshape(
        expert_count * capacity, model_width
    )
    picked = jnp.take(returned, slot_of, axis=0).astype(jnp.float32)
    branch = shared + jnp.sum(gate_values[:, :, None] * picked, axis=1)
    output = (middle + gate_mlp * branch).astype(jnp.bfloat16)
    out_grad = cotangent.astype(jnp.float32)
    grad_gate_mlp = out_grad * branch
    grad_branch = out_grad * gate_mlp
    grad_shared = grad_branch.astype(jnp.bfloat16)
    grad_picked = (gate_values[:, :, None] * grad_branch[:, None, :]).astype(jnp.bfloat16)
    grad_gates = jnp.sum(grad_branch[:, None, :] * picked, axis=2)
    grad_slots = jnp.einsum(
        "tks,tkd->sd", selector, grad_picked, preferred_element_type=jnp.float32
    )
    grad_slots = grad_slots.astype(jnp.bfloat16).reshape(expert_count, capacity, model_width)
    grad_owned = lax.all_to_all(grad_slots, "gx", split_axis=0, concat_axis=1, tiled=True)
    grad_inner = jnp.einsum(
        "ecd,efd->ecf", grad_owned, expert_back, preferred_element_type=jnp.float32
    )
    unused_inner, gelu_expert = jax.vjp(jax.nn.gelu, inner_pre)
    grad_inner_pre = gelu_expert(grad_inner)[0].astype(jnp.bfloat16)
    term_e_out = jnp.einsum(
        "ecf,ecd->efd", inner_act, grad_owned, preferred_element_type=jnp.float32
    )
    term_e_in = jnp.einsum(
        "ecd,ecf->edf", owned_rows, grad_inner_pre, preferred_element_type=jnp.float32
    )
    grad_rows = jnp.einsum(
        "ecf,edf->ecd", grad_inner_pre, expert_in, preferred_element_type=jnp.float32
    )
    grad_returned = (
        lax.all_to_all(
            grad_rows.astype(jnp.bfloat16), "gx", split_axis=1, concat_axis=0, tiled=True
        )
        .astype(grad_rows.dtype)
        .reshape(expert_count * capacity, model_width)
    )
    sum_e_in, sum_e_out = (
        lax.psum_scatter(
            term_e_in.astype(jnp.bfloat16), "gy", scatter_dimension=1, tiled=True
        ).astype(jnp.float32),
        lax.psum_scatter(
            term_e_out.astype(jnp.bfloat16), "gy", scatter_dimension=1, tiled=True
        ).astype(jnp.float32),
    )
    grad_chance = jnp.sum(chosen * grad_gates[:, :, None], axis=1)
    grad_logits = chance * (grad_chance - jnp.sum(grad_chance * chance, axis=-1, keepdims=True))
    grad_logits = grad_logits.astype(jnp.bfloat16)
    grad_hidden = dot_cols(grad_shared, fc2_full)
    unused_shared, gelu_shared = jax.vjp(jax.nn.gelu, hidden_pre)
    grad_hidden_pre = gelu_shared(grad_hidden)[0].astype(jnp.bfloat16)
    term_fc2 = dot_rows(hidden, grad_shared)
    term_fc1 = dot_rows(mixed_in, grad_hidden_pre)
    term_router = dot_rows(mixed_in, grad_logits)
    part_fc1, part_fc2, part_router = (
        lax.psum_scatter(
            term_fc1.astype(jnp.bfloat16), "gx", scatter_dimension=0, tiled=True
        ).astype(jnp.float32),
        lax.psum_scatter(
            term_fc2.astype(jnp.bfloat16), "gx", scatter_dimension=0, tiled=True
        ).astype(jnp.float32),
        lax.psum_scatter(
            term_router.astype(jnp.bfloat16), "gx", scatter_dimension=0, tiled=True
        ).astype(jnp.float32),
    )
    sum_fc1, sum_fc2, sum_router = (
        lax.psum_scatter(
            part_fc1.astype(jnp.bfloat16), "gy", scatter_dimension=0, tiled=True
        ).astype(jnp.float32),
        lax.psum_scatter(
            part_fc2.astype(jnp.bfloat16), "gy", scatter_dimension=0, tiled=True
        ).astype(jnp.float32),
        lax.psum_scatter(
            part_router.astype(jnp.bfloat16), "gy", scatter_dimension=0, tiled=True
        ).astype(jnp.float32),
    )
    grad_mixed = dot_cols(grad_hidden_pre, fc1_full) + dot_cols(grad_logits, router_full)
    grad_mixed = grad_mixed + jnp.sum(jnp.take(grad_returned, slot_of, axis=0), axis=1)
    unused_mix, mix_back = jax.vjp(modulate, middle, shift_mlp, scale_mlp)
    grad_mid_norm, grad_shift_mlp, grad_scale_mlp = mix_back(grad_mixed)
    grad_middle = out_grad + grad_mid_norm
    grad_gate_attn = grad_middle * attn_proj
    grad_proj = (grad_middle * gate_attn).astype(jnp.bfloat16)
    term_out = dot_rows(attn_low, grad_proj)
    grad_attn = (
        dot_cols(grad_proj, out_full).astype(jnp.bfloat16).reshape(tok_count, head_count, head_size)
    )
    grad_probs = jnp.einsum(
        "qhd,khd->hqk", grad_attn, value_rows, preferred_element_type=jnp.float32
    )
    grad_values = jnp.einsum(
        "hqk,qhd->khd", probs_low, grad_attn, preferred_element_type=jnp.float32
    )
    grad_scores = attn_probs * (
        grad_probs - jnp.sum(grad_probs * attn_probs, axis=-1, keepdims=True)
    )
    grad_scores = grad_scores.astype(jnp.bfloat16)
    grad_queries = (
        jnp.einsum("hqk,khd->qhd", grad_scores, key_rows, preferred_element_type=jnp.float32)
        * score_scale
    )
    grad_keys = (
        jnp.einsum("hqk,qhd->khd", grad_scores, queries, preferred_element_type=jnp.float32)
        * score_scale
    )
    grad_qkv = jnp.concatenate(
        [
            grad_queries.reshape(tok_count, model_width),
            grad_keys.reshape(tok_count, model_width),
            grad_values.reshape(tok_count, model_width),
        ],
        axis=1,
    ).astype(jnp.bfloat16)
    term_qkv = dot_rows(attn_in, grad_qkv)
    grad_attn_in = dot_cols(grad_qkv, qkv_full)
    unused_pre, pre_back = jax.vjp(modulate, residual, shift_attn, scale_attn)
    grad_input_norm, grad_shift_attn, grad_scale_attn = pre_back(grad_attn_in)
    d_tokens = grad_middle + grad_input_norm
    grad_token_mod = jnp.concatenate(
        [
            grad_shift_attn,
            grad_scale_attn,
            grad_gate_attn,
            grad_shift_mlp,
            grad_scale_mlp,
            grad_gate_mlp,
        ],
        axis=1,
    )
    grad_modulation = jnp.einsum("ti,tc->ic", member, grad_token_mod, precision=precise).astype(
        jnp.bfloat16
    )
    all_condition, all_modgrad = (
        lax.all_gather(condition, ("gx", "gy"), axis=0, tiled=True),
        lax.all_gather(grad_modulation, ("gx", "gy"), axis=0, tiled=True),
    )
    own_share = model_width // lax.axis_size(("gx", "gy"))
    own_start = lax.axis_index(("gx", "gy")) * own_share
    own_condition = lax.dynamic_slice_in_dim(all_condition, own_start, own_share, 1)
    owned_ada = dot_rows(own_condition, all_modgrad)
    attn_terms = (term_qkv, term_out)
    attn_parts = (
        lax.psum_scatter(
            attn_terms[0].astype(jnp.bfloat16), "gx", scatter_dimension=0, tiled=True
        ).astype(jnp.float32),
        lax.psum_scatter(
            attn_terms[1].astype(jnp.bfloat16), "gx", scatter_dimension=0, tiled=True
        ).astype(jnp.float32),
    )
    attn_sums = (
        lax.psum_scatter(
            attn_parts[0].astype(jnp.bfloat16), "gy", scatter_dimension=0, tiled=True
        ).astype(jnp.float32),
        lax.psum_scatter(
            attn_parts[1].astype(jnp.bfloat16), "gy", scatter_dimension=0, tiled=True
        ).astype(jnp.float32),
    )
    sum_qkv, sum_out = attn_sums
    return (
        output,
        d_tokens,
        owned_ada,
        sum_qkv,
        sum_out,
        sum_fc1,
        sum_fc2,
        sum_router,
        sum_e_in,
        sum_e_out,
    )


def solution(mesh):
    in_specs = (
        P(("gx", "gy"), None),
        P(("gx", "gy")),
        P(("gx", "gy"), None),
        P(("gx", "gy"), None),
        P(("gx", "gy"), None),
        P(("gx", "gy"), None),
        P(("gx", "gy"), None),
        P(("gx", "gy"), None),
        P(("gx", "gy"), None),
        P(("gx", "gy"), None),
        P(("gx", "gy"), None),
        P("gx", "gy", None),
        P("gx", "gy", None),
    )
    out_specs = (
        P(("gx", "gy"), None),
        P(("gx", "gy"), None),
        P(("gx", "gy"), None),
        P(("gx", "gy"), None),
        P(("gx", "gy"), None),
        P(("gx", "gy"), None),
        P(("gx", "gy"), None),
        P(("gx", "gy"), None),
        P("gx", "gy", None),
        P("gx", "gy", None),
    )
    step = by_slices if dict(mesh.shape) == {"gx": 2, "gy": 16} else by_weights
    return jax.shard_map(
        step, mesh=mesh, in_specs=in_specs, out_specs=out_specs, check_vma=False
    )
```

profile of v0, /device:TPU:0, one launch (start us, length us, event | category | flops | bytes accessed | tf_op | source)
XLA Modules:
  0.0 296.5 jit_solution(8384448507802896829)
XLA Ops:
  0.7 0.7 convert_element_type.11
  1.4 0.1 multiply_cosine_fusion
  1.5 0.3 convolution_bitcast_fusion
  1.8 0.7 pad.4.cond
  2.5 79.5 %front.1 = (bf16[4,768,384]{2,1,0:T(8,128)(2,1)}, bf16[768,192]{1,0:T(8,128)(2,1)}, bf16[4,384,768]{2,1,0:T(8,128)(2,1)}, bf16[192,768]{1,0:T(8,128)(2,1)}, bf16...) custom-call(s32[1,2]{1,0:T(1,128)} %lengths.3, ...), custom_call_target="tpu_custom_call" | custom-call | tf_op jit(solution)/shard_map/front/pallas_call | solution.py:522
  82.0 137.7 %block.1 = (f32[128,768]{1,0:T(8,128)}, f32[128,768]{1,0:T(8,128)}, f32[8,128]{1,0:T(8,128)}, bf16[4,8,48,384]{3,2,1,0:T(8,128)(2,1)}, f32[16,24,192]{2,1,0:T(8,...) custom-call(bf16[128,768]{1,0:T(8,128)(2,1)} %get-tuple-element.53.mixed, bf16[128,768]{1,0:T(8,128)(2,1)} %get-tuple-element.54.grad, ...), custom_call_target="tpu_custom_call" | custom-call | tf_op jit(solution)/shard_map/block/pallas_call | solution.py:768
  219.7 69.3 %rear.1 = (bf16[128,768]{1,0:T(8,128)(2,1)}, f32[128,768]{1,0:T(8,128)}, f32[24,4608]{1,0:T(8,128)}, f32[24,2304]{1,0:T(8,128)}, f32[24,768]{1,0:T(8,128)}, /*in...) custom-call(s32[1,2]{1,0:T(1,128)} %lengths.3, f32[128,768]{1,0:T(8,128)} %get-tuple-element.60.sum_branch, ...), custom_call_target="tpu_custom_call" | custom-call | tf_op jit(solution)/shard_map/rear/pallas_call | solution.py:999
  289.0 5.9 %finish.1 = (f32[4,48,3072]{2,1,0:T(8,128)}, f32[24,3072]{1,0:T(8,128)}, f32[8,128]{1,0:T(8,128)}, bf16[128,768]{1,0:T(8,128)(2,1)}, f32[128,768]{1,0:T(8,128)},...) custom-call(bf16[4,48,3072]{2,1,0:T(8,128)(2,1)} %get-tuple-element., ...), custom_call_target="tpu_custom_call" | custom-call | tf_op jit(solution)/shard_map/finish/pallas_call | solution.py:1068
  294.8 1.3 slice_bitcast_fusion
  (3 shorter events, 0.0 us)
where the time goes:
time: 301 us; the launch traced here: 297 us
  Pallas kernels  292 us (97%)
    pallas_call x1, Pallas kernels, block(): pl.pallas_call(block_kernel, out_shape=[shape((toks, model), f32), shape(...  138 us
    pallas_call x1, Pallas kernels, front(): pl.pallas_call(front_kernel, out_shape=(shape((experts, model, wide), bf)...  79.5 us
    pallas_call x1, Pallas kernels, rear(): pl.pallas_call(rear_kernel, out_shape=[shape((toks, model), bf), shape((t...  69.3 us

commit v1 on v0

--- a/solution.py
+++ b/solution.py
@@ -14,7 +14,7 @@
 ANY = pl.ANY
 VMEM = pltpu.VMEM
 DMA = pltpu.SemaphoreType.DMA
-LINE = (1, 3, 2)
+LINE = (1, 2, 3)
 
 precise = lax.Precision.HIGHEST
 layer_epsilon = 1e-06
@@ -31,6 +31,10 @@
 
 def chip(y, z, x):
     return 8 * y + 2 * z + x
+
+
+def along(z, step):
+    return z + step - 2 * (z % 2) * (step % 2) - 4 * (z // 2) * (step // 2)
 
 
 def meet(partners):
@@ -42,7 +46,7 @@
 
 def cross_partners(here):
     y, z, x, c = here
-    return [device(y, (z + step) % 4, x, c) for step in LINE] + [
+    return [device(y, along(z, step), x, c) for step in LINE] + [
         device(1 - y, z, x, c),
         device(y, z, 1 - x, c),
     ]
@@ -59,19 +63,29 @@
         self.here, self.y_first, self.own, self.slot = here, y_first, own, slot
         self.send, self.recv, self.pair, self.started = send, recv, pair, []
 
-    def copy(self, source, number, recv, to):
+    def number(self, a, step, b):
+        y, z, x, c = self.here
+        flip_y, flip_x = (a, b) if self.y_first else (b, a)
+        return chip(1 - y if flip_y else y, along(z, step), 1 - x if flip_x else x)
+
+    def copy(self, source, number, to, recv=None):
+        recv = self.recv if recv is None else recv
         sent = remote(source, self.slot(number), self.send.at[len(self.started)], recv.at[number], to)
         sent.start()
         self.started.append(sent)
 
-    def forward(self, source, number, to_y, to_x, to_pair=True):
+    def to_side(self, source, number, second):
         y, z, x, c = self.here
-        if to_y:
-            self.copy(source, number, self.recv, device(1 - y, z, x, c))
-        if to_x:
-            self.copy(source, number, self.recv, device(y, z, 1 - x, c))
-        if to_pair and self.pair is not None:
-            self.copy(source, number, self.pair, device(y, z, x, 1 - c))
+        self.copy(source, number, device(1 - y, z, x, c) if self.y_first != second else device(y, z, 1 - x, c))
+
+    def to_line(self, source, number, step):
+        y, z, x, c = self.here
+        self.copy(source, number, device(y, along(z, step), x, c))
+
+    def to_pair(self, source, number):
+        y, z, x, c = self.here
+        if self.pair is not None:
+            self.copy(source, number, device(y, z, x, 1 - c), self.pair)
 
     def arrive(self, number, recv=None):
         recv = self.recv if recv is None else recv
@@ -79,44 +93,38 @@
         remote(block, block, self.send.at[0], recv.at[number], device(*self.here)).wait_recv()
         return block
 
+    def start_first(self):
+        self.to_side(self.own, self.number(0, 0, 0), False)
+        self.to_pair(self.own, self.number(0, 0, 0))
+
     def start_line(self, step):
-        y, z, x, c = self.here
-        self.copy(self.own, chip(y, z, x), self.recv, device(y, (z + step) % 4, x, c))
-
-    def start_first(self):
-        y, z, x, c = self.here
-        self.forward(self.own, chip(y, z, x), self.y_first, not self.y_first)
+        self.to_line(self.own, self.number(0, 0, 0), step)
 
     def start_last(self):
-        y, z, x, c = self.here
-        self.forward(self.own, chip(y, z, x), not self.y_first, self.y_first, False)
+        self.to_side(self.own, self.number(0, 0, 0), True)
 
     def line_first(self, step):
-        y, z, x, c = self.here
-        number = chip(y, (z + step) % 4, x)
-        self.forward(self.arrive(number), number, self.y_first, not self.y_first)
+        number = self.number(0, step, 0)
+        block = self.arrive(number)
+        if step == 2:
+            self.to_line(block, number, 1)
+        self.to_side(block, number, False)
+        self.to_pair(block, number)
 
     def line_last(self, step):
-        y, z, x, c = self.here
-        number = chip(y, (z + step) % 4, x)
-        self.forward(self.slot(number), number, not self.y_first, self.y_first, False)
+        number = self.number(0, step, 0)
+        self.to_side(self.slot(number), number, True)
 
     def second(self, step):
-        y, z, x, c = self.here
-        if self.y_first:
-            number = chip(1 - y, (z + step) % 4, x)
-        else:
-            number = chip(y, (z + step) % 4, 1 - x)
-        self.forward(self.arrive(number), number, not self.y_first, self.y_first)
+        number = self.number(1, step, 0)
+        block = self.arrive(number)
+        self.to_side(block, number, True)
+        self.to_pair(block, number)
 
     def third(self, step):
-        y, z, x, c = self.here
-        for other in (0, 1):
-            if self.y_first:
-                number = chip(y if other == 0 else 1 - y, (z + step) % 4, 1 - x)
-            else:
-                number = chip(1 - y, (z + step) % 4, x if other == 0 else 1 - x)
-            self.forward(self.arrive(number), number, False, False)
+        for a in (0, 1):
+            number = self.number(a, step, 1)
+            self.to_pair(self.arrive(number), number)
 
     def finish(self):
         for sent in self.started:
@@ -129,13 +137,11 @@
 def gather_start(gathers):
     for gather in gathers:
         gather.start_first()
-    for gather in gathers:
-        gather.start_line(1)
-        gather.start_line(3)
+    for step in (1, 2):
+        for gather in gathers:
+            gather.start_line(step)
     for gather in gathers:
         gather.start_last()
-    for gather in gathers:
-        gather.start_line(2)
 
 
 def gather_line(gathers, step):
@@ -170,14 +176,14 @@
 
 
 class Scatter:
-    def __init__(self, here, y_first, part, got, send, recv):
-        self.here, self.y_first, self.part, self.got = here, y_first, part, got
+    def __init__(self, here, y_first, part, got, send, recv, relay=False):
+        self.here, self.y_first, self.part, self.got, self.relay = here, y_first, part, got, relay
         self.send, self.recv, self.started = send, recv, []
 
     def number(self, a, b, step):
         y, z, x, c = self.here
         flip_y, flip_x = (a, b) if self.y_first else (b, a)
-        return chip(1 - y if flip_y else y, (z + step) % 4, 1 - x if flip_x else x)
+        return chip(1 - y if flip_y else y, along(z, step), 1 - x if flip_x else x)
 
     def toward(self, second):
         y, z, x, c = self.here
@@ -212,12 +218,14 @@
         y, z, x, c = self.here
         number = self.number(0, 0, step)
         self.add(number, 8 + step)
+        if self.relay and step == 2:
+            self.add(number, 14)
         if step:
-            self.copy(self.part(number), 11 + step, device(y, (z + step) % 4, x, c))
+            self.copy(self.part(number), 11 + step, device(y, along(z, 1 if self.relay and step == 3 else step), x, c))
 
     def total(self):
         result = self.part(self.number(0, 0, 0))[...].astype(jnp.float32)
-        for step in (1, 2, 3):
+        for step in (1, 2) if self.relay else (1, 2, 3):
             result = result + self.arrive(11 + step)[...].astype(jnp.float32)
         return result
 
@@ -226,23 +234,20 @@
             sent.wait_send()
 
 
-def scatter_all(scatters, between):
-    order = (2, 1, 3, 0)
+def scatter_all(scatters, more, between):
+    order = (3, 2, 1, 0)
+    for turn, step in enumerate(order):
+        for b in (1, 0):
+            for scatter in scatters:
+                scatter.one(b, step)
+        if turn + 2 < 4:
+            more(order[turn + 2])
+        if turn:
+            for scatter in scatters:
+                scatter.two(order[turn - 1])
+        between(turn)
     for scatter in scatters:
-        scatter.first(order[0])
-    for scatter in scatters:
-        scatter.first(order[1])
-    for turn, step in enumerate(order):
-        for scatter in scatters:
-            scatter.one(1, step)
-        for scatter in scatters:
-            scatter.one(0, step)
-        if turn + 2 < 4:
-            for scatter in scatters:
-                scatter.first(order[turn + 2])
-        for scatter in scatters:
-            scatter.two(step)
-        between(turn)
+        scatter.two(order[3])
 
 
 def nt(a, b):
@@ -289,9 +294,8 @@
 
 
 def own_modulation(here, mod, item, half, part):
-    y, z, x, c = here
+    first = 2 * here[3]
     model = item.shape[1]
-    first = 8 * y + 4 * x + 2 * c
     at = slice(part * model, (part + 1) * model)
     return jnp.where(item, mod[half, pl.ds(first + 1, 1), at], mod[half, pl.ds(first, 1), at])
 
@@ -302,21 +306,21 @@
 
 
 def front_kernel(
-    lengths, tokens, cotangent, routes, cond, w_ada, w_qkv, w_out, w_router, w_fc1, e1, e2, f2,
-    w1, w1s, w2, w2s, qkv_w, out_w, conds, mod, mixed, grad, gates, attn_in, qkv, probs, attn_low, attn_proj, middle, chance,
-    square, f1, s_got, s_rows, q_full, o_full, q_fold, o_fold, q_stage, o_stage, q_block, o_block, c_buf, part, sib, z_part, z_got, xy_part, xy_got,
-    pre_send, pre_recv, g_send, g_recv, g_pair, a_send, a_recv, a_pair_send, a_pair, b_send, b_recv, b_pair, l_sem, d_send, d_recv,
-    c_send, c_recv, m_send, m_recv,
+    lengths, tokens, cotangent, routes, cond, w_ada, w_qkv, w_out, w_router, w_fc1, e1,
+    w1, w1s_out, qkv_w, out_w, mod_out, mixed_out, grad_out, gates_out, attn_in_out, qkv_out, probs_out, attn_low_out, attn_proj_out, middle_out, chance_out,
+    w1s, mod, mixed, grad, gates, attn_in, qkv, probs, attn_low, attn_proj, middle, chance,
+    square, strip_own, f1, s_got, s_rows, q_full, o_full, a_full, q_fold, o_fold, a_fold, q_stage, o_stage, a_stage, q_block, o_block, c_buf, z_part, z_got,
+    pre_send, pre_recv, g_send, g_recv, g_pair, a_send, a_recv, a_pair_send, a_pair, b_send, b_recv, b_pair, l_sem, o_sem,
+    c_send, c_recv, m_send, m_recv, r_send, r_recv,
 ):
     here = y, z, x, c = place()
     me, k, gy = chip(y, z, x), 2 * z + x, 4 * z + 2 * x + c
     rows, model = w_out.shape
     others = [(dy, dz, dx) for dy in (0, 1) for dz in (0, 1, 2, 3) for dx in (0, 1) if (dy, dz, dx) != (0, 0, 0)]
-    spot = lambda dy, dz, dx: (1 - y if dy else y, (z + dz) % 4, 1 - x if dx else x)
+    spot = lambda dy, dz, dx: (1 - y if dy else y, along(z, dz), 1 - x if dx else x)
     sibling = device(y, z, x, 1 - c)
-    peers = [(*spot(dy, dz, dx), c if same else 1 - c) for same in (True, False) for dy, dz, dx in [(0, 0, 0)] + others]
-    peers = peers[1:]
-    meet([device(*peer) for peer in peers])
+    crossed = [device(y, along(z, step), x, 1 - c) for step in LINE]
+    meet([device(*spot(*o), c) for o in others] + [sibling] + crossed)
 
     started = []
 
@@ -324,19 +328,18 @@
         copy.start()
         started.append(copy)
 
-    number = 2 * me + c
-    for i, peer in enumerate(peers):
-        go(remote(cond.at[2 * chip(*peer[:3]) + peer[3]], c_buf.at[number], c_send.at[i], c_recv.at[number], device(*peer)))
+    for i, (step, core) in enumerate([(0, 1 - c)] + [(step, core) for step in LINE for core in (c, 1 - c)]):
+        go(remote(cond.at[along(z, step)], c_buf.at[z, c], c_send.at[i], c_recv.at[z, c], device(y, along(z, step), x, core)))
 
     mine = pl.ds(pl.multiple_of(rows * c, 8), rows)
     square[...] = jnp.zeros_like(square)
     square[0 : w_router.shape[0], 0:rows] = wide_float(w_router[...])
     router = square[...].T[:rows]
-    for w, fold, stage, i in ((w_qkv, q_fold, q_stage, 0), (w_out, o_fold, o_stage, 1)):
+    for i, (w, fold, stage) in enumerate(((w_ada, a_fold, a_stage), (w_qkv, q_fold, q_stage), (w_out, o_fold, o_stage))):
         cut = w.shape[1] // 2
         for h in (0, 1):
             fold[h, :, :cut] = wide_float(w[:, h * cut : (h + 1) * cut])
-            if i:
+            if i == 2:
                 fold[h, :, cut:] = router
         go(remote(fold.at[1 - c], stage.at[mine, :], pre_send.at[i], pre_recv.at[i], sibling))
         stage[mine, :] = fold[c]
@@ -344,30 +347,42 @@
     depth, width = e1.shape[1], w1.shape[2]
     cols = lambda n: pl.ds(pl.multiple_of(width * n, 128), width)
     strip = lambda n: pl.ds(pl.multiple_of(depth * n, 16), depth)
-    half2, half2s = e2.shape[1], f2.shape[0]
-    at2 = lambda core: pl.ds(pl.multiple_of(half2 * core, 16), half2)
-    at2s = lambda core: pl.ds(pl.multiple_of(half2s * core, 16), half2s)
-    local = [
-        pltpu.make_async_copy(e1.at[:, :, cols(k)], w1.at[:, strip(gy), :], l_sem.at[0]),
-        pltpu.make_async_copy(e2, w2.at[:, at2(c), :], l_sem.at[1]),
-        pltpu.make_async_copy(f2, w2s.at[at2s(c), :], l_sem.at[2]),
-    ]
-    for copy in local:
-        copy.start()
+    load = pltpu.make_async_copy(e1.at[:, :, cols(k)], strip_own, l_sem.at[0])
+    load.start()
     plane = [o for o in others if o[0] == 0]
 
-    def send_experts(steps):
+    def send_experts(steps, aside):
         for i, o in enumerate(plane):
-            if o[1] in steps:
+            if o[1] in steps and o[2] == aside:
                 ty, tz, tx = spot(*o)
                 go(remote(e1.at[:, :, cols(2 * tz + tx)], w1.at[:, strip(gy), :], a_send.at[i], a_recv.at[k], device(ty, tz, tx, c)))
 
-    send_experts((0, 1))
-
-    for i, (stage, block) in enumerate(((q_stage, q_block), (o_stage, o_block))):
+    send_experts((1,), 0)
+
+    def folded(i, stage):
         theirs = stage.at[pl.ds(pl.multiple_of(rows * (1 - c), 8), rows), :]
         remote(theirs, theirs, pre_send.at[i], pre_recv.at[i], sibling).wait_recv()
-        block[...] = low(stage[...])
+        return low(stage[...])
+
+    block = folded(0, a_stage)
+    width_a = a_full.shape[3]
+    number = 2 * y + x
+    to_y, to_x = device(1 - y, z, x, c), device(y, z, 1 - x, c)
+    for i in (0, 1):
+        a_full[i, number] = block[:, i * width_a : (i + 1) * width_a]
+
+    def send_a(i, n, lane, to):
+        go(remote(a_full.at[i, n], a_full.at[i, n], r_send.at[i, lane], r_recv.at[i, n], to))
+
+    def wait_a(i, n):
+        remote(a_full.at[i, n], a_full.at[i, n], r_send.at[0, 0], r_recv.at[i, n], sibling).wait_recv()
+
+    for i in (0, 1):
+        send_a(i, number, 0, to_x)
+    for i in (0, 1):
+        send_a(i, number, 1, to_y)
+    q_block[...] = folded(1, q_stage)
+    o_block[...] = folded(2, o_stage)
     gathers = []
     for i, (block, full, y_first) in enumerate(((q_block, q_full, False), (o_block, o_full, True))):
         slot = functools.partial(lambda full, n: full.at[c, pl.ds(pl.multiple_of(2 * rows * n, 16), 2 * rows), :], full)
@@ -375,29 +390,29 @@
         slot(me)[...] = block[...]
     gather_start(gathers)
 
-    c_buf[number] = cond[number]
-    for peer in peers:
-        block = c_buf.at[2 * chip(*peer[:3]) + peer[3]]
-        remote(block, block, c_send.at[0], c_recv.at[2 * chip(*peer[:3]) + peer[3]], sibling).wait_recv()
-    for gz in range(4):
-        for gy_ in range(2):
-            group = [c_buf[2 * chip(gy_, gz, gx_) + core] for gx_ in (0, 1) for core in (0, 1)]
-            conds[pl.ds(8 * (2 * gz + gy_), 8), :] = group[0] + group[1] + group[2] + group[3]
-    lhs = low(conds[...])[:, :rows]
-    for h in (0, 1):
-        at = slice(h * part.shape[2], (h + 1) * part.shape[2])
-        part[h] = nn(lhs, w_ada[:, at])
-    go(remote(part.at[1 - c], sib, m_send.at[0], m_recv.at[0], sibling))
-
+    n_y, n_x = 2 * (1 - y) + x, 2 * y + 1 - x
+    n_xy = 2 * (1 - y) + 1 - x
+    for i in (0, 1):
+        wait_a(i, n_x)
+        send_a(i, n_x, 2, to_y)
     gather_second(gathers, 0)
-    remote(sib, sib, m_send.at[0], m_recv.at[0], sibling).wait_recv()
-    for gz in range(4):
-        at = slice(16 * gz, 16 * (gz + 1))
-        z_part[gz] = part[c, at, :] + sib[at, :]
+
+    c_buf[z, c] = cond[z]
+    for step, core in [(0, 1 - c)] + [(step, core) for step in LINE for core in (c, 1 - c)]:
+        block = c_buf.at[along(z, step), core]
+        remote(block, block, c_send.at[0], c_recv.at[along(z, step), core], sibling).wait_recv()
+    lhs = low(jnp.concatenate([c_buf[i, 0] + c_buf[i, 1] for i in range(4)], axis=0))[:, : 8 * rows]
+    for i in (0, 1):
+        wait_a(i, n_y)
+        wait_a(i, n_xy)
+        term = nn(lhs, a_full[i].reshape(8 * rows, width_a))
+        for line in range(4):
+            z_part[line, 4 * i : 4 * (i + 1), :] = term[8 * line : 8 * line + 4]
     for step in LINE:
-        go(remote(z_part.at[(z + step) % 4], z_got.at[step - 1], m_send.at[step], m_recv.at[step], device(y, (z + step) % 4, x, c)))
+        at = along(z, step)
+        go(remote(z_part.at[at], z_got.at[step - 1], m_send.at[step], m_recv.at[step], device(y, at, x, c)))
+    send_experts((2, 3), 0)
     gather_line(gathers, 1)
-    send_experts((3,))
     slim = w1s.shape[1]
     for n in range(16):
         block = wide_float(w_fc1[:, slim * n : slim * (n + 1)])
@@ -407,30 +422,18 @@
         go(remote(f1.at[chip(ty, tz, tx)], s_got.at[c, me], b_send.at[i], b_recv.at[me], device(ty, tz, tx, c)))
     s_got[c, me] = f1[me]
     gather_second(gathers, 1)
-    gather_line(gathers, 3)
-    send_experts((2,))
-    total = wide_float(z_part[z])
+    gather_line(gathers, 2)
+    send_experts((0, 1, 2, 3), 1)
+    total = z_part[z]
     for step in LINE:
         remote(z_got.at[step - 1], z_got.at[step - 1], m_send.at[0], m_recv.at[step], sibling).wait_recv()
-        total = total + wide_float(z_got[step - 1])
-    xy_part[0] = total
-    go(remote(xy_part.at[0], xy_got.at[0], m_send.at[4], m_recv.at[4], device(y, z, 1 - x, c)))
+        total = total + z_got[step - 1]
+    mod[c] = jnp.concatenate([total, pltpu.roll(total, 4, 0)], axis=1)
+    go(remote(mod.at[c], mod.at[c], m_send.at[0], m_recv.at[0], sibling))
+    gather_second(gathers, 2)
+    gather_line(gathers, 3)
     gather_second(gathers, 3)
-    remote(xy_got.at[0], xy_got.at[0], m_send.at[0], m_recv.at[4], sibling).wait_recv()
-    xy_part[1] = xy_part[0] + xy_got[0]
-    go(remote(xy_part.at[1], xy_got.at[1], m_send.at[5], m_recv.at[5], device(1 - y, z, x, c)))
-    gather_line(gathers, 2)
-    remote(xy_got.at[1], xy_got.at[1], m_send.at[0], m_recv.at[5], sibling).wait_recv()
-    mod[c] = xy_part[1] + xy_got[1]
-    go(remote(mod.at[c], mod.at[c], m_send.at[6], m_recv.at[6], sibling))
-    gather_second(gathers, 2)
-    twin = [
-        remote(e2, w2.at[:, at2(c), :], d_send.at[0], d_recv.at[0], sibling),
-        remote(f2, w2s.at[at2s(c), :], d_send.at[1], d_recv.at[1], sibling),
-    ]
-    for copy in twin:
-        go(copy)
-    remote(mod.at[1 - c], mod.at[1 - c], m_send.at[0], m_recv.at[6], sibling).wait_recv()
+    remote(mod.at[1 - c], mod.at[1 - c], m_send.at[0], m_recv.at[0], sibling).wait_recv()
 
     item = item_mask(lengths, tokens.shape)
     residual = wide_float(tokens[...])
@@ -441,27 +444,18 @@
         gather_third(gathers, step)
     for gather in gathers:
         gather.finish()
-    keep = [pltpu.make_async_copy(q_full, qkv_w, l_sem.at[4]), pltpu.make_async_copy(o_full, out_w, l_sem.at[5])]
-    for copy in keep:
-        copy.start()
+    keep = []
+
+    def leave(source, target):
+        keep.append(pltpu.make_async_copy(source, target, o_sem.at[len(keep)]))
+        keep[-1].start()
+
+    leave(q_full, qkv_w)
+    leave(o_full, out_w)
 
     cut = q_full.shape[2]
     for h in (0, 1):
         qkv[:, h * cut : (h + 1) * cut] = low(nn(attn_in[...], q_full[h]))
-
-    for copy in local:
-        copy.wait()
-    for i, o in enumerate([(0, 0, 0)] + [o for step in (0, 1, 3, 2) for o in plane if o[1] == step]):
-        _, sz, sx = spot(*o)
-        source = 2 * sz + sx
-        block = w1.at[:, strip(2 * source + c), :]
-        if i:
-            remote(block, block, a_send.at[0], a_recv.at[source], sibling).wait_recv()
-        go(remote(block, block, a_pair_send.at[i], a_pair.at[source], sibling))
-    for o in others:
-        n = chip(*spot(*o))
-        remote(s_got.at[c, n], s_got.at[c, n], b_send.at[0], b_recv.at[n], sibling).wait_recv()
-    go(remote(s_got.at[c], s_got.at[c], b_pair.at[0], b_pair.at[1], sibling))
 
     side = wide_float(item[:, :128])
     same = side == side.T
@@ -489,9 +483,27 @@
     turned = jnp.where(choices(routes, square), chance[...], 0.0).T[:8]
     high = low(turned)
     gates[...] = jnp.concatenate([high, low(turned - wide_float(high))], axis=0)
-
-    for copy in keep:
-        copy.wait()
+    for source, target in (
+        (mixed, mixed_out), (grad, grad_out), (gates, gates_out), (mod, mod_out), (attn_in, attn_in_out), (qkv, qkv_out), (probs, probs_out),
+        (attn_low, attn_low_out), (attn_proj, attn_proj_out), (middle, middle_out), (chance, chance_out),
+    ):
+        leave(source, target)
+
+    load.wait()
+    leave(strip_own, w1.at[:, strip(gy), :])
+    for i, o in enumerate([(0, 0, 0)] + [o for step in (0, 1, 3, 2) for o in plane if o[1] == step]):
+        _, sz, sx = spot(*o)
+        source = 2 * sz + sx
+        block = w1.at[:, strip(2 * source + c), :]
+        if i:
+            remote(block, block, a_send.at[0], a_recv.at[source], sibling).wait_recv()
+        go(remote(block if i else strip_own, block, a_pair_send.at[i], a_pair.at[source], sibling))
+    for o in others:
+        n = chip(*spot(*o))
+        remote(s_got.at[c, n], s_got.at[c, n], b_send.at[0], b_recv.at[n], sibling).wait_recv()
+    go(remote(s_got.at[c], s_got.at[c], b_pair.at[0], b_pair.at[1], sibling))
+
+
     for copy in started:
         copy.wait_send()
     for source in range(8):
@@ -501,65 +513,63 @@
     for n in range(32):
         s_rows[n * rows : (n + 1) * rows, :] = wide_float(s_got[n % 2, n // 2])[:rows]
     w1s[...] = low(s_rows[...])
-    remote(w2.at[:, at2(1 - c), :], w2.at[:, at2(1 - c), :], d_send.at[0], d_recv.at[0], sibling).wait_recv()
-    remote(w2s.at[at2s(1 - c), :], w2s.at[at2s(1 - c), :], d_send.at[1], d_recv.at[1], sibling).wait_recv()
-
-
-def front(lengths, tokens, cotangent, routes, condition, w_ada, w_qkv, w_out, w_router, w_fc1, w_fc2, e_fc1, e_fc2):
+    leave(w1s, w1s_out)
+    for copy in keep:
+        copy.wait()
+
+
+def front(lengths, tokens, cotangent, routes, condition, w_ada, w_qkv, w_out, w_router, w_fc1, e_fc1):
     rows, model = w_out.shape
     toks = tokens.shape[0]
-    y, z, x, c = place()
-    cond = condition.astype(jnp.float32).reshape(-1, 32, rows).transpose(1, 0, 2)
-    spot = jnp.arange(8) == (4 * x + 2 * c + jnp.arange(2))[:, None]
-    cond = jnp.einsum("dir,is->dsr", cond, spot.astype(jnp.float32), precision=precise)
-    cond = jnp.pad(cond, ((0, 0), (0, 0), (0, 128 - rows)))
+    c = place()[3]
+    cond = condition.astype(jnp.float32).reshape(2, 2, 4, 2, 2, rows).transpose(2, 0, 1, 3, 4, 5).reshape(4, 2, 8 * rows)
+    spot = jnp.arange(8) == (2 * c + jnp.arange(2))[:, None]
+    cond = jnp.einsum("zil,is->zsl", cond, spot.astype(jnp.float32), precision=precise)
+    cond = jnp.pad(cond, ((0, 0), (0, 0), (0, -8 * rows % 128)))
     ff = w_fc1.shape[1]
     slim, wide = ff // 16, ff // 8
     experts = e_fc1.shape[0]
     bf, f32 = jnp.bfloat16, jnp.float32
     shape = jax.ShapeDtypeStruct
     q_half, o_half, a_half = w_qkv.shape[1] // 2, w_out.shape[1] // 2 + 128, w_ada.shape[1] // 2
+    shapes = (
+        shape((experts, model, wide), bf),
+        shape((model, slim), bf),
+        shape((2, model, q_half), bf),
+        shape((2, model, o_half), bf),
+        shape((2, 8, a_half), f32),
+        shape((toks, model), bf),
+        shape((toks, model), bf),
+        shape((16, toks), bf),
+        shape((toks, model), bf),
+        shape((toks, 3 * model), bf),
+        shape((HEADS, toks, toks), f32),
+        shape((toks, model), bf),
+        shape((toks, model), f32),
+        shape((toks, model), f32),
+        shape((toks, 128), f32),
+    )
     result = pl.pallas_call(
         front_kernel,
-        out_shape=(
-            shape((experts, model, wide), bf),
-            shape((model, slim), bf),
-            shape((experts, 2 * e_fc2.shape[1], model), bf),
-            shape((2 * w_fc2.shape[0], model), bf),
-            shape((2, model, q_half), bf),
-            shape((2, model, o_half), bf),
-            shape((64, 128), f32),
-            shape((2, 16, a_half), f32),
-            shape((toks, model), bf),
-            shape((toks, model), bf),
-            shape((16, toks), bf),
-            shape((toks, model), bf),
-            shape((toks, 3 * model), bf),
-            shape((HEADS, toks, toks), f32),
-            shape((toks, model), bf),
-            shape((toks, model), f32),
-            shape((toks, model), f32),
-            shape((toks, 128), f32),
-        ),
+        out_shape=shapes,
         in_specs=[pl.BlockSpec(memory_space=pltpu.SMEM)]
         + [pl.BlockSpec(memory_space=VMEM)] * 9
-        + [pl.BlockSpec(memory_space=ANY)] * 3,
-        out_specs=[pl.BlockSpec(memory_space=ANY), pl.BlockSpec(memory_space=VMEM)]
-        + [pl.BlockSpec(memory_space=ANY)] * 4
-        + [pl.BlockSpec(memory_space=VMEM)] * 12,
-        scratch_shapes=[
-            VMEM((128, 128), f32), VMEM((16, 32, slim), bf), VMEM((2, 16, 32, slim), bf), VMEM((model, slim), f32),
-            VMEM((2, model, q_half), bf), VMEM((2, model, o_half), bf),
-            VMEM((2, rows, q_half), f32), VMEM((2, rows, o_half), f32), VMEM((2 * rows, q_half), f32), VMEM((2 * rows, o_half), f32),
+        + [pl.BlockSpec(memory_space=ANY)],
+        out_specs=[pl.BlockSpec(memory_space=ANY)] * 15,
+        scratch_shapes=[VMEM(a.shape, a.dtype) for a in (shapes[1], *shapes[4:])]
+        + [
+            VMEM((128, 128), f32), VMEM((experts, e_fc1.shape[1], wide), bf), VMEM((16, 32, slim), bf), VMEM((2, 16, 32, slim), bf), VMEM((model, slim), f32),
+            VMEM((2, model, q_half), bf), VMEM((2, model, o_half), bf), VMEM((2, 4, 2 * rows, a_half // 2), bf),
+            VMEM((2, rows, q_half), f32), VMEM((2, rows, o_half), f32), VMEM((2, rows, a_half), f32),
+            VMEM((2 * rows, q_half), f32), VMEM((2 * rows, o_half), f32), VMEM((2 * rows, a_half), f32),
             VMEM((2 * rows, q_half), bf), VMEM((2 * rows, o_half), bf),
-            VMEM((32, 8, 128), f32), VMEM((2, 64, a_half), f32), VMEM((64, a_half), f32),
-            VMEM((4, 16, a_half), f32), VMEM((3, 16, a_half), f32), VMEM((2, 16, a_half), f32), VMEM((2, 16, a_half), f32),
-            DMA((2,)), DMA((2,)), DMA((2, 31)), DMA((2, 16)), DMA((2, 16)), DMA((7,)), DMA((8,)), DMA((8,)), DMA((8,)),
-            DMA((15,)), DMA((16,)), DMA((2,)), DMA((6,)), DMA((2,)), DMA((2,)), DMA((31,)), DMA((32,)), DMA((7,)), DMA((7,)),
+            VMEM((4, 2, 8, cond.shape[2]), f32), VMEM((4, 8, a_half // 2), f32), VMEM((3, 8, a_half // 2), f32),
+            DMA((3,)), DMA((3,)), DMA((2, 31)), DMA((2, 16)), DMA((2, 16)), DMA((7,)), DMA((8,)), DMA((8,)), DMA((8,)),
+            DMA((15,)), DMA((16,)), DMA((2,)), DMA((1,)), DMA((15,)), DMA((7,)), DMA((4, 2)), DMA((4,)), DMA((4,)), DMA((2, 3)), DMA((2, 4)),
         ],
         compiler_params=pltpu.CompilerParams(collective_id=1, has_side_effects=True, vmem_limit_bytes=62 << 20),
         name="front",
-    )(lengths, tokens, cotangent, routes.T, cond, w_ada, w_qkv, w_out, w_router.T, w_fc1, e_fc1, e_fc2, w_fc2)
+    )(lengths, tokens, cotangent, routes.T, cond, w_ada, w_qkv, w_out, w_router.T, w_fc1, e_fc1)
     return result
 
 
@@ -624,14 +634,14 @@
 
 def block_kernel(
     mixed, grad, gates, w1_in, w1s_in, w2_in, w2s_in,
-    sum_branch, sum_back, sum_gc, own1, own1s, own2, own2s,
-    X, G, gt, w1, w1s, w2, w2s, act, pre, act_s, pre_s, tile_sum, tile_back,
+    sum_branch, sum_back, sum_gc, out1, out1s, out2, out2s,
+    own1, own1s, own2, own2s, X, G, gt, w1, w1s, w2, w2s, act, pre, act_s, pre_s, tile_sum, tile_back,
     p_branch, p_back, p_gc, r_branch, r_back, r_gc, d1, d1s, d2, d2s, from1, from1s, from2, from2s,
-    l_sem, g_send, g_recv, send, recv, t_send, t_recv,
+    l_sem, o_sem, g_send, g_recv, send, recv, t_send, t_recv, w_send, w_recv,
 ):
     here = y, z, x, c = place()
     me = chip(y, z, x)
-    spot = lambda dy, dz, dx: (1 - y if dy else y, (z + dz) % 4, 1 - x if dx else x)
+    spot = lambda dy, dz, dx: (1 - y if dy else y, along(z, dz), 1 - x if dx else x)
     sibling = device(y, z, x, 1 - c)
     experts = w1.shape[0]
     meet(cross_partners(here) + [sibling])
@@ -642,8 +652,13 @@
         gathers.append(Gather(here, y_first, block, slot, g_send.at[i], g_recv.at[i]))
         local.append(pltpu.make_async_copy(block, slot(me), l_sem.at[i]))
     gather_start(gathers)
-    for i, (source, target) in enumerate(((w1_in, w1), (w1s_in, w1s), (w2_in, w2), (w2s_in, w2s))):
+    half2, half2s = w2_in.shape[1], w2s_in.shape[0]
+    own2_at = w2.at[:, pl.ds(pl.multiple_of(half2 * c, 16), half2), :]
+    own2s_at = w2s.at[pl.ds(pl.multiple_of(half2s * c, 16), half2s), :]
+    for i, (source, target) in enumerate(((w1_in, w1), (w1s_in, w1s), (w2_in, own2_at), (w2s_in, own2s_at))):
         local.append(pltpu.make_async_copy(source, target, l_sem.at[3 + i]))
+    for i, (source, target) in enumerate(((w2_in, own2_at), (w2s_in, own2s_at))):
+        local.append(remote(source, target, w_send.at[i], w_recv.at[i], sibling))
     for copy in local:
         copy.start()
 
@@ -677,22 +692,21 @@
     for copy in local:
         copy.wait()
     tile(0, 0)
-    gather_line(gathers, 3)
+    gather_line(gathers, 2)
     tile(0, 1)
     gather_third(gathers, 1)
     tile(1, 0)
+    gather_second(gathers, 2)
+    tile(1, 1)
+    gather_line(gathers, 3)
+    gather_third(gathers, 2)
+    tile(2, 0)
     gather_second(gathers, 3)
-    tile(1, 1)
-    gather_line(gathers, 2)
+    tile(2, 1)
+    back_first(2)
+    back_first(1)
     gather_third(gathers, 3)
     tile(3, 0)
-    gather_second(gathers, 2)
-    back_first(1)
-    tile(3, 1)
-    back_first(3)
-    gather_third(gathers, 2)
-    tile(2, 0)
-    tile(2, 1)
 
     def back_one(step):
         for scatter in scatters:
@@ -706,6 +720,12 @@
 
     flat = lambda value: value.reshape(value.shape[0] * value.shape[1], value.shape[2])
     twins = [None] * (2 * experts)
+    leaving = []
+
+    def leave(source, target):
+        leaving.append(pltpu.make_async_copy(source, target, o_sem.at[len(leaving)]))
+        leaving[-1].start()
+
 
     def weight(e):
         d1[e] = tn(flat(X[...]), flat(pre[e])).astype(jnp.bfloat16).reshape(d1.shape[1:])
@@ -719,18 +739,21 @@
         own1[e] = (d1[e, :, c].astype(jnp.float32) + from1[e].astype(jnp.float32)).astype(jnp.bfloat16)
         twins[2 * e + 1].wait()
         own2[e] = d2[e, c].astype(jnp.float32) + from2[e].astype(jnp.float32)
-
+        leave(own1.at[e], out1.at[e])
+        leave(own2.at[e], out2.at[e])
+
+    back_one(2)
+    tile(3, 1)
+    back_first(3)
+    back_two(2)
     back_one(1)
-    back_first(2)
+    weight(0)
     back_two(1)
-    weight(0)
+    home(0)
+    back_first(0)
+    weight(1)
     back_one(3)
     back_two(3)
-    home(0)
-    weight(1)
-    back_one(2)
-    back_first(0)
-    back_two(2)
     home(1)
     weight(2)
     home(2)
@@ -744,20 +767,25 @@
     home(3)
     back_one(0)
     twin1s.wait()
-    own1s[...] = d1s[:, c] + from1s[...]
+    total = d1s[:, c] + from1s[...]
+    own1s[...] = low(jnp.concatenate([total, jnp.zeros((16, own1s.shape[1] - total.shape[1], total.shape[2]), jnp.float32)], axis=1))
     twin2s.wait()
     own2s[...] = d2s[c].astype(jnp.float32) + from2s[...].astype(jnp.float32)
+    leave(own1s, out1s)
+    leave(own2s, out2s)
     back_two(0)
     sum_branch[...] = scatters[0].total()
     sum_back[...] = scatters[1].total()
     sum_gc[...] = scatters[2].total()
+    for copy in leaving:
+        copy.wait()
     for gather in gathers:
         gather.finish()
     for scatter in scatters:
         scatter.finish()
 
 
-def block(mixed, grad, gates, w1, w1s, w2, w2s):
+def block(mixed, grad, gates, w1, w1s, e_fc2, w_fc2):
     bf, f32 = jnp.bfloat16, jnp.float32
     toks, model = mixed.shape
     experts, _, wide = w1.shape
@@ -772,15 +800,16 @@
             shape((toks, model), f32),
             shape((8, 128), f32),
             shape((experts, 8, 2 * rows, wide), bf),
-            shape((16, rows, slim), f32),
+            shape((16, 32, slim), bf),
             shape((experts, wide // 2, model), f32),
             shape((slim // 2, model), f32),
         ],
         in_specs=[pl.BlockSpec(memory_space=VMEM)] * 3 + [pl.BlockSpec(memory_space=ANY)] * 4,
-        out_specs=[pl.BlockSpec(memory_space=VMEM)] * 7,
+        out_specs=[pl.BlockSpec(memory_space=VMEM)] * 3 + [pl.BlockSpec(memory_space=ANY)] * 4,
         scratch_shapes=[
+            VMEM((experts, 8, 2 * rows, wide), bf), VMEM((16, 32, slim), bf), VMEM((experts, wide // 2, model), f32), VMEM((slim // 2, model), f32),
             blocks(model), blocks(model), VMEM((16, 16, 128), bf),
-            VMEM(w1.shape, bf), VMEM(w1s.shape, bf), VMEM(w2.shape, bf), VMEM(w2s.shape, bf),
+            VMEM(w1.shape, bf), VMEM(w1s.shape, bf), VMEM((experts, wide, model), bf), VMEM((slim, model), bf),
             VMEM((experts, 16, toks, wide), bf), VMEM((experts, 16, toks, wide), bf), blocks(slim), blocks(slim),
             VMEM((4 * toks, model), f32), VMEM((4 * toks, model), f32),
             blocks(model), blocks(model), VMEM((16, 8, 128), f32),
@@ -789,29 +818,29 @@
             VMEM((experts, 2, wide // 2, model), bf), VMEM((2, slim // 2, model), bf),
             VMEM((experts, 8, 2 * rows, wide), bf), VMEM((16, rows, slim), f32),
             VMEM((experts, wide // 2, model), bf), VMEM((slim // 2, model), bf),
-            DMA((7,)), DMA((3, 15)), DMA((3, 16)), DMA((3, 15)), DMA((3, 15)), DMA((2 * experts + 2,)), DMA((2 * experts + 2,)),
+            DMA((7,)), DMA((2 * experts + 2,)), DMA((3, 15)), DMA((3, 16)), DMA((3, 15)), DMA((3, 15)), DMA((2 * experts + 2,)), DMA((2 * experts + 2,)),
+            DMA((2,)), DMA((2,)),
         ],
         compiler_params=pltpu.CompilerParams(collective_id=2, has_side_effects=True, vmem_limit_bytes=62 << 20),
         name="block",
-    )(mixed, grad, gates, w1, w1s, w2, w2s)
-
-
-def rear_kernel(
-    lengths, sum_branch, sum_back, sum_gc, tokens, cotangent, routes, mod, conds, mixed, attn_in, qkv, probs, attn_low, attn_proj, middle,
-    chance, qkv_in, out_in, part1, part1s,
-    output, d_tokens, d_ada, d_qkv, d_out, d_router, own1, own1s,
-    square, q_w, o_w, grad_attn, grad_qkv, grad_mid, o_mine, o_got, q_mine, q_got, part_o, part_a, part_b,
-    got_o, got_a, got_b, fin, mod_tile, all_mod,
-    l_sem, s_send, s_recv, send, recv, g_send, g_recv, g_pair, f_send, f_recv, a_send, a_recv, b_send, b_recv,
-):
+    )(mixed, grad, gates, w1, w1s, e_fc2, w_fc2)
+
+
+def rear_kernel(lengths, *refs):
+    incoming, refs = refs[:16], refs[16:]
+    (qkv_in, out_in, part1, part1s, output, d_tokens, d_ada, d_qkv, d_out, d_router, own1, own1s), refs = refs[:12], refs[12:]
+    (sum_branch, sum_back, sum_gc, tokens, cotangent, routes, condition, mod, mixed, attn_in, qkv, probs, attn_low, attn_proj, middle, chance), refs = refs[:16], refs[16:]
+    (square, strip_own, slice_own, q_w, o_w, grad_attn, grad_qkv, grad_mid, o_mine, o_got, q_mine, q_got, part_o, part_a, part_b, got_o, got_a, got_b, fin, mod_tile, all_mod, l_sem, s_send, s_recv, send, recv, g_send, g_recv, g_pair, f_send, f_recv, a_send, a_recv, b_send, b_recv, i_sem) = refs
     here = y, z, x, c = place()
     me, k = chip(y, z, x), 2 * z + x
     sibling = device(y, z, x, 1 - c)
     others = [(dy, dz, dx) for dy in (0, 1) for dz in (0, 1, 2, 3) for dx in (0, 1) if (dy, dz, dx) != (0, 0, 0)]
     plane = [o for o in others if o[0] == 0]
-    spot = lambda dy, dz, dx: (1 - y if dy else y, (z + dz) % 4, 1 - x if dx else x)
+    spot = lambda dy, dz, dx: (1 - y if dy else y, along(z, dz), 1 - x if dx else x)
+    held = (sum_branch, sum_back, sum_gc, tokens, cotangent, routes, condition, mod, mixed, attn_in, qkv, probs, attn_low, attn_proj, middle, chance)
+    loads = [pltpu.make_async_copy(a, b, i_sem.at[i]) for i, (a, b) in enumerate(zip(incoming, held))]
     local = [pltpu.make_async_copy(qkv_in, q_w, l_sem.at[0]), pltpu.make_async_copy(out_in, o_w, l_sem.at[1])]
-    for copy in local:
+    for copy in loads + local:
         copy.start()
     meet([device(*spot(*o), c) for o in others] + [sibling])
     started = []
@@ -822,15 +851,22 @@
 
     wide = part1.shape[3]
     columns = lambda n: own1.at[:, :, pl.ds(pl.multiple_of(wide * n, 128), wide)]
-    home = [pltpu.make_async_copy(part1.at[:, k], columns(k), l_sem.at[2]), pltpu.make_async_copy(part1s.at[me], own1s.at[me], l_sem.at[3])]
+    home = [pltpu.make_async_copy(part1.at[:, k], strip_own, l_sem.at[2]), pltpu.make_async_copy(part1s.at[me], slice_own, l_sem.at[3])]
     for copy in home:
         copy.start()
-    for i, o in enumerate(plane):
-        ty, tz, tx = spot(*o)
-        go(remote(part1.at[:, 2 * tz + tx], columns(k), a_send.at[i], a_recv.at[k], device(ty, tz, tx, c)))
+
+    def send_experts(aside):
+        for i, o in enumerate(plane):
+            if o[2] == aside:
+                ty, tz, tx = spot(*o)
+                go(remote(part1.at[:, 2 * tz + tx], columns(k), a_send.at[i], a_recv.at[k], device(ty, tz, tx, c)))
+
+    send_experts(0)
     for i, o in enumerate(others):
         go(remote(part1s.at[chip(*spot(*o))], own1s.at[me], b_send.at[i], b_recv.at[me], device(*spot(*o), c)))
 
+    for copy in loads:
+        copy.wait()
     item = item_mask(lengths, tokens.shape)
     first = ~item
     model = item.shape[1]
@@ -852,8 +888,11 @@
     share = chance[...]
     grad_logits = low(share * (grad_chance - jnp.sum(grad_chance * share, axis=-1, keepdims=True)))
     term_router = tn(mixed[...], grad_logits)
-    for copy in local:
+    for copy in local + home:
         copy.wait()
+    home = [pltpu.make_async_copy(strip_own, columns(k), l_sem.at[2]), pltpu.make_async_copy(slice_own, own1s.at[me], l_sem.at[3])]
+    for copy in home:
+        copy.start()
     grad_mixed = sum_back[...] + nt(grad_logits, o_w[0, :, cut:])
     normed, scale = norm(middle[...])
     per_item(3, grad_mixed)
@@ -873,24 +912,14 @@
     for i, (part, got, y_first) in enumerate(((part_o, got_o, False), (part_a, got_a, True), (part_b, got_b, False))):
         take = functools.partial(lambda ref, n: ref.at[n], part)
         land = functools.partial(lambda ref, n: ref.at[n], got)
-        scatters.append(Scatter(here, y_first, take, land, send.at[i], recv.at[i]))
-
-    def out_stage(stage):
-        tool = scatters[0]
-        if stage == 0:
-            swap_o.wait()
-            for n in range(16):
-                at = slice(n * rows, (n + 1) * rows)
-                part_o[n] = low(wide_float(o_mine[c, at, :]) + wide_float(o_got[at, :]))
-            for step in (2, 1, 3, 0):
-                tool.first(step)
-        else:
-            for step in ((2,), (1, 3), (0,))[stage - 1]:
-                tool.one(1, step)
-                tool.one(0, step)
-        if stage > 1:
-            for step in ((2,), (1, 3))[stage - 2]:
-                tool.two(step)
+        scatters.append(Scatter(here, y_first, take, land, send.at[i], recv.at[i], relay=True))
+
+    swap_o.wait()
+    for n in range(16):
+        at = slice(n * rows, (n + 1) * rows)
+        part_o[n] = low(wide_float(o_mine[c, at, :]) + wide_float(o_got[at, :]))
+    for step in (3, 2, 1, 0):
+        scatters[0].first(step)
 
     left, sides = head_lanes()
     for pair in range(model // 128):
@@ -905,38 +934,50 @@
             outs.append((nn(grad_scores, key) * 0.125, tn(grad_scores, q) * 0.125, tn(low(prob), ga)))
         for base, one, two in zip((0, model, 2 * model), *outs):
             grad_qkv[:, base + 128 * pair : base + 128 * (pair + 1)] = low(jnp.where(left, one, two))
-        if pair in (1, 3, 5):
-            out_stage(pair // 2)
 
     third = q_w.shape[2]
     for h in (0, 1):
         q_mine[h] = low(tn(attn_in[...], grad_qkv[:, h * third : (h + 1) * third]))
-    swap_q = remote(q_mine.at[1 - c], q_got, s_send.at[1], s_recv.at[1], sibling)
-    swap_q.start()
-    out_stage(3)
+    swap_q = {}
+    for step in (3, 2, 1, 0):
+        for side in (0, 1):
+            at = pl.ds(pl.multiple_of(2 * rows * (4 * side + along(z, step)), 16), 2 * rows)
+            i = 1 + 2 * step + side
+            swap_q[step, side] = remote(q_mine.at[1 - c, at, :], q_got.at[at, :], s_send.at[i], s_recv.at[i], sibling)
+            swap_q[step, side].start()
+    send_experts(1)
     grad_in = nt(grad_qkv[:, :third], q_w[0]) + nt(grad_qkv[:, third:], q_w[1])
     normed, scale = norm(wide_float(tokens[...]))
     per_item(0, grad_in)
     per_item(1, grad_in * normed)
     d_tokens[...] = grad_mid[...] + norm_back(grad_in * (1.0 + modulation(0, 1)), normed, scale)
-    rows16[12] = jnp.zeros((4, model), jnp.float32)
-    mod_tile[...] = low(jnp.concatenate([rows16[i] for i in range(13)], axis=0))
+    rows16[12] = wide_float(condition[...])
+    rows16[13] = jnp.zeros((2, model), jnp.float32)
+    mod_tile[...] = low(jnp.concatenate([rows16[i] for i in range(14)], axis=0))
 
     slot = lambda n: all_mod.at[n, c]
-    spread = Gather(here, True, mod_tile, slot, g_send, g_recv, g_pair)
+    spread = Gather(here, False, mod_tile, slot, g_send, g_recv, g_pair)
     all_mod[me, c] = mod_tile[...]
     gather_start([spread])
-    swap_q.wait()
     edge = part_a.shape[2]
-    for n in range(16):
-        at = slice(n * rows, (n + 1) * rows)
-        total = low(wide_float(q_mine[c, at, :]) + wide_float(q_got[at, :]))
-        part_a[n] = total[:, :edge]
-        part_b[n] = total[:, edge:]
+
+    def fold(step):
+        for side in (0, 1):
+            swap_q[step, side].wait()
+            first_n = 8 * side + 2 * along(z, step)
+            for n in (first_n, first_n + 1):
+                at = pl.ds(pl.multiple_of(rows * n, 16), rows)
+                total = low(wide_float(q_mine[c, at, :]) + wide_float(q_got[at, :]))
+                part_a[n] = total[:, :edge]
+                part_b[n] = total[:, edge:]
+        for scatter in scatters[1:]:
+            scatter.first(step)
+
+    fold(3)
+    fold(2)
 
     def turn(at):
         if at == 0:
-            scatters[0].two(0)
             spread.second(0)
             for step in LINE:
                 gather_line([spread], step)
@@ -947,25 +988,26 @@
             for step in (0,) + LINE:
                 spread.third(step)
             spread.finish()
-
-    scatter_all(scatters[1:], turn)
+        else:
+            flat = all_mod[...].reshape(32 * 16, model)
+            share_rows = rows // 2
+            own = (2 * me + c) * share_rows
+            source = lax.broadcasted_iota(jnp.int32, (model, 128), 0)
+            lane = lax.broadcasted_iota(jnp.int32, (model, 128), 1)
+            own_columns = nn(flat, low(wide_float((source == own + lane) & (lane < share_rows))))
+            row = lax.broadcasted_iota(jnp.int32, (512, 128), 0) % 16
+            own_columns = jnp.where((row >= 12) & (row < 14), own_columns, 0.0)
+            for part in range(6):
+                lhs = low(pltpu.roll(own_columns, 512 + 2 * part - 12, 0))
+                d_ada[:, part * model : (part + 1) * model] = tn(lhs, flat)[:share_rows]
+
+    scatter_all(scatters, fold, turn)
     fin[c] = jnp.concatenate([scatters[1].total(), scatters[2].total(), scatters[0].total()], axis=1)
     half = rows // 2
     mine = pl.ds(pl.multiple_of(half * c, 8), half)
     theirs = pl.ds(pl.multiple_of(half * (1 - c), 8), half)
     swap = remote(fin.at[c, theirs, :], fin.at[c, theirs, :], f_send, f_recv, sibling)
     swap.start()
-
-    flat = all_mod[...].reshape(32 * 16, model)
-    row = lax.broadcasted_iota(jnp.int32, (64, 512), 1)
-    spot_of = row // 16
-    place_of = 16 * ((spot_of // 4) % 4) + 8 * (spot_of // 16) + 4 * ((spot_of // 2) % 2) + 2 * (spot_of % 2) + row % 2
-    meets = lax.broadcasted_iota(jnp.int32, (64, 512), 0) == place_of
-    columns_in = low(conds[...])
-    for part in range(6):
-        pick = low(wide_float(meets & ((row % 16) // 2 == part)))
-        lhs = low(tn(columns_in, pick))
-        d_ada[:, part * model : (part + 1) * model] = nn(lhs, flat)[: d_ada.shape[0]]
 
     for i, o in enumerate(plane):
         n = 2 * spot(*o)[1] + spot(*o)[2]
@@ -988,13 +1030,14 @@
     d_router[half:, :] = jnp.zeros((128 - half, 128), jnp.float32)
 
 
-def rear(lengths, sums, tokens, cotangent, routes, saved, qkv_w, out_w, part1, part1s):
+def rear(lengths, sums, tokens, cotangent, routes, condition, saved, qkv_w, out_w, part1, part1s):
     bf, f32 = jnp.bfloat16, jnp.float32
     toks, model = tokens.shape
     rows = model // 16
     experts, _, depth, wide = part1.shape
     q_half, o_half = qkv_w.shape[2], out_w.shape[2]
     a_half = model
+    incoming = (*sums, tokens, cotangent, routes.T, condition, *saved)
     shape = jax.ShapeDtypeStruct
     return pl.pallas_call(
         rear_kernel,
@@ -1006,26 +1049,25 @@
             shape((rows // 2, model), f32),
             shape((128, 128), f32),
             shape((experts, depth, 8 * wide), bf),
-            shape(part1s.shape, f32),
+            shape(part1s.shape, bf),
         ],
-        in_specs=[pl.BlockSpec(memory_space=pltpu.SMEM)]
-        + [pl.BlockSpec(memory_space=VMEM)] * 16
-        + [pl.BlockSpec(memory_space=ANY)] * 4,
+        in_specs=[pl.BlockSpec(memory_space=pltpu.SMEM)] + [pl.BlockSpec(memory_space=ANY)] * 20,
         out_specs=[pl.BlockSpec(memory_space=VMEM)] * 6 + [pl.BlockSpec(memory_space=ANY)] * 2,
-        scratch_shapes=[
-            VMEM((128, 128), f32), VMEM(qkv_w.shape, bf), VMEM(out_w.shape, bf),
+        scratch_shapes=[VMEM(a.shape, a.dtype) for a in incoming]
+        + [
+            VMEM((128, 128), f32), VMEM((experts, depth, wide), bf), VMEM(part1s.shape[1:], bf), VMEM(qkv_w.shape, bf), VMEM(out_w.shape, bf),
             VMEM((toks, model), bf), VMEM((toks, 3 * model), bf), VMEM((toks, model), f32),
             VMEM((2, model, o_half), bf), VMEM((model, o_half), bf),
             VMEM((2, model, q_half), bf), VMEM((model, q_half), bf),
             VMEM((16, rows, o_half), bf), VMEM((16, rows, a_half), bf), VMEM((16, rows, q_half - a_half), bf),
             VMEM((15, rows, o_half), bf), VMEM((15, rows, a_half), bf), VMEM((15, rows, q_half - a_half), bf),
             VMEM((2, rows, q_half + o_half), f32), VMEM((16, model), bf), VMEM((16, 2, 16, model), bf),
-            DMA((4,)), DMA((2,)), DMA((2,)), DMA((3, 15)), DMA((3, 15)), DMA((31,)), DMA((16,)), DMA((16,)), DMA, DMA,
-            DMA((7,)), DMA((8,)), DMA((15,)), DMA((16,)),
+            DMA((4,)), DMA((9,)), DMA((9,)), DMA((3, 15)), DMA((3, 15)), DMA((31,)), DMA((16,)), DMA((16,)), DMA, DMA,
+            DMA((7,)), DMA((8,)), DMA((15,)), DMA((16,)), DMA((16,)),
         ],
         compiler_params=pltpu.CompilerParams(collective_id=3, has_side_effects=True, vmem_limit_bytes=62 << 20),
         name="rear",
-    )(lengths, *sums, tokens, cotangent, routes.T, *saved, qkv_w, out_w, part1, part1s)
+    )(lengths, *incoming, qkv_w, out_w, part1, part1s)
 
 
 def finish_kernel(*refs):
@@ -1053,21 +1095,22 @@
     loads[2].wait()
     slim = slices.shape[2]
     for n in range(slices.shape[0] // 2):
-        fc1[:, 2 * n * slim : 2 * (n + 1) * slim] = jnp.concatenate([slices[2 * n], slices[2 * n + 1]], axis=1)
+        pair = [wide_float(slices[2 * n + i])[: fc1.shape[0]] for i in (0, 1)]
+        fc1[:, 2 * n * slim : 2 * (n + 1) * slim] = jnp.concatenate(pair, axis=1)
     store(fc1, outputs[1])
-    outputs[2][...] = router[...].T[: outputs[2].shape[0]]
+    outputs[2][...] = router[...].T[: outputs[2].shape[0], : outputs[2].shape[1]]
     for copy in stores:
         copy.wait()
 
 
 def finish(own1, own1s, d_router, *others):
     f32 = jnp.float32
-    rows = own1s.shape[1]
+    rows = own1.shape[1] // 2
     wide = (rows, own1s.shape[0] * own1s.shape[2])
     shape = jax.ShapeDtypeStruct
     result = pl.pallas_call(
         finish_kernel,
-        out_shape=[shape(own1.shape, f32), shape(wide, f32), shape((8, 128), f32)] + [shape(a.shape, a.dtype) for a in others],
+        out_shape=[shape(own1.shape, f32), shape(wide, f32), shape((8, rows), f32)] + [shape(a.shape, a.dtype) for a in others],
         in_specs=[pl.BlockSpec(memory_space=ANY)] * (3 + len(others)),
         out_specs=[pl.BlockSpec(memory_space=ANY)] * 2
         + [pl.BlockSpec(memory_space=VMEM)]
@@ -1077,7 +1120,7 @@
         compiler_params=pltpu.CompilerParams(vmem_limit_bytes=62 << 20),
         name="finish",
     )(own1, own1s, d_router, *others)
-    return result[0], result[1], result[2][:, :rows].T, *result[3:]
+    return result[0], result[1], result[2].T, *result[3:]
 
 
 def layer_norm(values):
@@ -1136,14 +1179,14 @@
 ):
     model_width = tokens.shape[1]
     condition = jax.nn.silu(sinusoid(timesteps, model_width)).astype(jnp.bfloat16)
-    (w1, w1s, w2, w2s, qkv_w, out_w, conds, mod, mixed, grad, gates, attn_in, qkv, probs, attn_low, attn_proj, middle,
+    (w1, w1s, qkv_w, out_w, mod, mixed, grad, gates, attn_in, qkv, probs, attn_low, attn_proj, middle,
      chance) = front(
-        lengths, tokens, cotangent, routes, condition, w_ada, w_qkv, w_out, w_router, w_fc1, w_fc2, e_fc1, e_fc2
-    )
-    *sums, part1, part1s, d_e2, d_fc2 = block(mixed, grad, gates, w1, w1s, w2, w2s)
-    saved = (mod, conds, mixed, attn_in, qkv, probs, attn_low, attn_proj, middle, chance)
+        lengths, tokens, cotangent, routes, condition, w_ada, w_qkv, w_out, w_router, w_fc1, e_fc1
+    )
+    *sums, part1, part1s, d_e2, d_fc2 = block(mixed, grad, gates, w1, w1s, e_fc2, w_fc2)
+    saved = (mod, mixed, attn_in, qkv, probs, attn_low, attn_proj, middle, chance)
     output, d_tokens, d_ada, d_qkv, d_out, d_router, own1, own1s = rear(
-        lengths, sums, tokens, cotangent, routes, saved, qkv_w, out_w, part1, part1s
+        lengths, sums, tokens, cotangent, routes, condition, saved, qkv_w, out_w, part1, part1s
     )
     d_e1, d_fc1, d_router, output, d_tokens, d_ada, d_qkv, d_out, d_fc2, d_e2 = finish(
         own1, own1s, d_router, output, d_tokens, d_ada, d_qkv, d_out, d_fc2, d_e2

time: 301 us -> 273 us (0.907)
  Pallas kernels: 292 us -> 264 us
    pallas_call x1, Pallas kernels: 79.5 us -> 65 us  [front(): pl.pallas_call(front_kernel, out_shape=shapes, in_specs=[pl.BlockSpec(mem...]
    pallas_call x1, Pallas kernels: 69.3 us -> 58.9 us  [rear(): pl.pallas_call(rear_kernel, out_shape=[shape((toks, model), bf), shape((t...]
where the time goes in v1:
time: 273 us; the launch traced here: 268 us
  Pallas kernels  264 us (97%)
    pallas_call x1, Pallas kernels, block(): pl.pallas_call(block_kernel, out_shape=[shape((toks, model), f32), shape(...  135 us
    pallas_call x1, Pallas kernels, front(): pl.pallas_call(front_kernel, out_shape=shapes, in_specs=[pl.BlockSpec(mem...  65 us
    pallas_call x1, Pallas kernels, rear(): pl.pallas_call(rear_kernel, out_shape=[shape((toks, model), bf), shape((t...  58.9 us
    pallas_call x1, Pallas kernels, finish(): pl.pallas_call(finish_kernel, out_shape=[shape(own1.shape, f32), shape(wi...  5.71 us

profile of v1, /device:TPU:0, one launch (start us, length us, event | category | flops | bytes accessed | tf_op | source)
XLA Modules:
  0.0 268.2 jit_solution(550065708806547478)
XLA Ops:
  0.7 0.7 convert_element_type.12
  1.3 0.3 multiply_cosine_fusion
  1.7 0.1 reshape.63
  1.8 0.3 convolution_bitcast_fusion
  2.1 0.6 pad.4.cond
  2.7 65.0 %front.1 = (bf16[4,768,384]{2,1,0:T(8,128)(2,1)}, bf16[768,192]{1,0:T(8,128)(2,1)}, bf16[2,768,1152]{2,1,0:T(8,128)(2,1)}, bf16[2,768,512]{2,1,0:T(8,128)(2,1)},...) custom-call(s32[1,2]{1,0:T(1,128)} %lengths.3, ...), custom_call_target="tpu_custom_call" | custom-call | tf_op jit(solution)/shard_map/front/pallas_call | solution.py:552
  67.7 134.7 %block.1 = (f32[128,768]{1,0:T(8,128)}, f32[128,768]{1,0:T(8,128)}, f32[8,128]{1,0:T(8,128)}, bf16[4,8,48,384]{3,2,1,0:T(8,128)(2,1)}, bf16[16,32,192]{2,1,0:T(8...) custom-call(bf16[128,768]{1,0:T(8,128)(2,1)} %get-tuple-element.50.mixed.refs_8_, ...), custom_call_target="tpu_custom_call" | custom-call | tf_op jit(solution)/shard_map/block/pallas_call | solution.py:796
  202.3 0.1 multiply_cosine_fusion.1
  202.5 0.6 fusion.2.refs_6_
  203.1 58.9 %rear.1 = (bf16[128,768]{1,0:T(8,128)(2,1)}, f32[128,768]{1,0:T(8,128)}, f32[24,4608]{1,0:T(8,128)}, f32[24,2304]{1,0:T(8,128)}, f32[24,768]{1,0:T(8,128)}, /*in...) custom-call(s32[1,2]{1,0:T(1,128)} %lengths.3, f32[128,768]{1,0:T(8,128)} %get-tuple-element.55.refs_0_, ...), custom_call_target="tpu_custom_call" | custom-call | tf_op jit(solution)/shard_map/rear/pallas_call | solution.py:1042
  262.0 5.7 %finish.1 = (f32[4,48,3072]{2,1,0:T(8,128)}, f32[24,3072]{1,0:T(8,128)}, f32[8,24]{1,0:T(8,128)}, bf16[128,768]{1,0:T(8,128)(2,1)}, f32[128,768]{1,0:T(8,128)}, ...) custom-call(bf16[4,48,3072]{2,1,0:T(8,128)(2,1)} %get-tuple-element., ...), custom_call_target="tpu_custom_call" | custom-call | tf_op jit(solution)/shard_map/finish/pallas_call | solution.py:1111
  (4 shorter events, 0.1 us)

commit v2 on v1

--- a/solution.py
+++ b/solution.py
@@ -3,6 +3,7 @@
 
 import jax
 import jax.numpy as jnp
+import numpy as np
 from jax import lax
 from jax.experimental import pallas as pl
 from jax.experimental.pallas import tpu as pltpu
@@ -300,16 +301,29 @@
     return jnp.where(item, mod[half, pl.ds(first + 1, 1), at], mod[half, pl.ds(first, 1), at])
 
 
+def frequencies(model_width):
+    half = model_width // 2
+    return np.tile(np.exp(-math.log(10000.0) * np.arange(half) / half).astype(np.float32), 2)
+
+
+def conditions(steps, shape, first, column, half, frequency):
+    row = lax.broadcasted_iota(jnp.int32, shape, 0) - first
+    angle = jnp.where(row == 0, wide_float(steps[0]), wide_float(steps[1])) * frequency
+    wave = jnp.where(column < half, jnp.cos(angle), jnp.sin(angle))
+    value = wave / (1.0 + jnp.exp(-wave))
+    return wide_float(low(jnp.where((row == 0) | (row == 1), value, 0.0)))
+
+
 def head_lanes():
     lane = lax.broadcasted_iota(jnp.int32, (1, 128), 1)
     return lane < 64, [low(wide_float(lane < 64)), low(wide_float(lane >= 64))]
 
 
 def front_kernel(
-    lengths, tokens, cotangent, routes, cond, w_ada, w_qkv, w_out, w_router, w_fc1, e1,
+    lengths, steps, tokens, cotangent, routes, waves, w_ada, w_qkv, w_out, w_router, w_fc1, e1,
     w1, w1s_out, qkv_w, out_w, mod_out, mixed_out, grad_out, gates_out, attn_in_out, qkv_out, probs_out, attn_low_out, attn_proj_out, middle_out, chance_out,
     w1s, mod, mixed, grad, gates, attn_in, qkv, probs, attn_low, attn_proj, middle, chance,
-    square, strip_own, f1, s_got, s_rows, q_full, o_full, a_full, q_fold, o_fold, a_fold, q_stage, o_stage, a_stage, q_block, o_block, c_buf, z_part, z_got,
+    square, cond, strip_own, f1, s_got, s_rows, q_full, o_full, a_full, q_fold, o_fold, a_fold, q_stage, o_stage, a_stage, q_block, o_block, c_buf, z_part, z_got,
     pre_send, pre_recv, g_send, g_recv, g_pair, a_send, a_recv, a_pair_send, a_pair, b_send, b_recv, b_pair, l_sem, o_sem,
     c_send, c_recv, m_send, m_recv, r_send, r_recv,
 ):
@@ -328,6 +342,10 @@
         copy.start()
         started.append(copy)
 
+    lane = lax.broadcasted_iota(jnp.int32, cond.shape[1:], 1)
+    for at in range(4):
+        column = model // 2 * (lane // (4 * rows)) + 4 * rows * at + lane % (4 * rows)
+        cond[at] = jnp.where(lane < 8 * rows, conditions(steps, cond.shape[1:], 2 * c, column, model // 2, waves[at : at + 1, :]), 0.0)
     for i, (step, core) in enumerate([(0, 1 - c)] + [(step, core) for step in LINE for core in (c, 1 - c)]):
         go(remote(cond.at[along(z, step)], c_buf.at[z, c], c_send.at[i], c_recv.at[z, c], device(y, along(z, step), x, core)))
 
@@ -377,10 +395,10 @@
     def wait_a(i, n):
         remote(a_full.at[i, n], a_full.at[i, n], r_send.at[0, 0], r_recv.at[i, n], sibling).wait_recv()
 
-    for i in (0, 1):
-        send_a(i, number, 0, to_x)
-    for i in (0, 1):
-        send_a(i, number, 1, to_y)
+    send_a(0, number, 0, to_y)
+    send_a(1, number, 0, to_x)
+    send_a(0, number, 1, to_x)
+    send_a(1, number, 1, to_y)
     q_block[...] = folded(1, q_stage)
     o_block[...] = folded(2, o_stage)
     gathers = []
@@ -392,9 +410,10 @@
 
     n_y, n_x = 2 * (1 - y) + x, 2 * y + 1 - x
     n_xy = 2 * (1 - y) + 1 - x
-    for i in (0, 1):
-        wait_a(i, n_x)
-        send_a(i, n_x, 2, to_y)
+    wait_a(0, n_y)
+    send_a(0, n_y, 2, to_x)
+    wait_a(1, n_x)
+    send_a(1, n_x, 2, to_y)
     gather_second(gathers, 0)
 
     c_buf[z, c] = cond[z]
@@ -402,8 +421,8 @@
         block = c_buf.at[along(z, step), core]
         remote(block, block, c_send.at[0], c_recv.at[along(z, step), core], sibling).wait_recv()
     lhs = low(jnp.concatenate([c_buf[i, 0] + c_buf[i, 1] for i in range(4)], axis=0))[:, : 8 * rows]
-    for i in (0, 1):
-        wait_a(i, n_y)
+    for i, n_last in enumerate((n_x, n_y)):
+        wait_a(i, n_last)
         wait_a(i, n_xy)
         term = nn(lhs, a_full[i].reshape(8 * rows, width_a))
         for line in range(4):
@@ -424,15 +443,15 @@
     gather_second(gathers, 1)
     gather_line(gathers, 2)
     send_experts((0, 1, 2, 3), 1)
+    gather_second(gathers, 2)
+    gather_line(gathers, 3)
+    gather_second(gathers, 3)
     total = z_part[z]
     for step in LINE:
         remote(z_got.at[step - 1], z_got.at[step - 1], m_send.at[0], m_recv.at[step], sibling).wait_recv()
         total = total + z_got[step - 1]
     mod[c] = jnp.concatenate([total, pltpu.roll(total, 4, 0)], axis=1)
     go(remote(mod.at[c], mod.at[c], m_send.at[0], m_recv.at[0], sibling))
-    gather_second(gathers, 2)
-    gather_line(gathers, 3)
-    gather_second(gathers, 3)
     remote(mod.at[1 - c], mod.at[1 - c], m_send.at[0], m_recv.at[0], sibling).wait_recv()
 
     item = item_mask(lengths, tokens.shape)
@@ -489,6 +508,12 @@
     ):
         leave(source, target)
 
+    for o in others:
+        n = chip(*spot(*o))
+        remote(s_got.at[c, n], s_got.at[c, n], b_send.at[0], b_recv.at[n], sibling).wait_recv()
+    go(remote(s_got.at[c], s_got.at[c], b_pair.at[0], b_pair.at[1], sibling))
+
+
     load.wait()
     leave(strip_own, w1.at[:, strip(gy), :])
     for i, o in enumerate([(0, 0, 0)] + [o for step in (0, 1, 3, 2) for o in plane if o[1] == step]):
@@ -498,34 +523,25 @@
         if i:
             remote(block, block, a_send.at[0], a_recv.at[source], sibling).wait_recv()
         go(remote(block if i else strip_own, block, a_pair_send.at[i], a_pair.at[source], sibling))
-    for o in others:
-        n = chip(*spot(*o))
-        remote(s_got.at[c, n], s_got.at[c, n], b_send.at[0], b_recv.at[n], sibling).wait_recv()
-    go(remote(s_got.at[c], s_got.at[c], b_pair.at[0], b_pair.at[1], sibling))
-
-
+    remote(s_got.at[1 - c], s_got.at[1 - c], b_pair.at[0], b_pair.at[1], sibling).wait_recv()
+    for n in range(32):
+        s_rows[n * rows : (n + 1) * rows, :] = wide_float(s_got[n % 2, n // 2])[:rows]
+    w1s[...] = low(s_rows[...])
+    leave(w1s, w1s_out)
     for copy in started:
         copy.wait_send()
     for source in range(8):
         block = w1.at[:, strip(2 * source + 1 - c), :]
         remote(block, block, a_send.at[0], a_pair.at[source], sibling).wait_recv()
-    remote(s_got.at[1 - c], s_got.at[1 - c], b_pair.at[0], b_pair.at[1], sibling).wait_recv()
-    for n in range(32):
-        s_rows[n * rows : (n + 1) * rows, :] = wide_float(s_got[n % 2, n // 2])[:rows]
-    w1s[...] = low(s_rows[...])
-    leave(w1s, w1s_out)
     for copy in keep:
         copy.wait()
 
 
-def front(lengths, tokens, cotangent, routes, condition, w_ada, w_qkv, w_out, w_router, w_fc1, e_fc1):
+def front(lengths, timesteps, tokens, cotangent, routes, w_ada, w_qkv, w_out, w_router, w_fc1, e_fc1):
     rows, model = w_out.shape
     toks = tokens.shape[0]
-    c = place()[3]
-    cond = condition.astype(jnp.float32).reshape(2, 2, 4, 2, 2, rows).transpose(2, 0, 1, 3, 4, 5).reshape(4, 2, 8 * rows)
-    spot = jnp.arange(8) == (2 * c + jnp.arange(2))[:, None]
-    cond = jnp.einsum("zil,is->zsl", cond, spot.astype(jnp.float32), precision=precise)
-    cond = jnp.pad(cond, ((0, 0), (0, 0), (0, -8 * rows % 128)))
+    waves = frequencies(model).reshape(2, 4, 4 * rows).transpose(1, 0, 2).reshape(4, 8 * rows)
+    waves = np.pad(waves, ((0, 0), (0, -8 * rows % 128)))
     ff = w_fc1.shape[1]
     slim, wide = ff // 16, ff // 8
     experts = e_fc1.shape[0]
@@ -552,24 +568,24 @@
     result = pl.pallas_call(
         front_kernel,
         out_shape=shapes,
-        in_specs=[pl.BlockSpec(memory_space=pltpu.SMEM)]
+        in_specs=[pl.BlockSpec(memory_space=pltpu.SMEM)] * 2
         + [pl.BlockSpec(memory_space=VMEM)] * 9
         + [pl.BlockSpec(memory_space=ANY)],
         out_specs=[pl.BlockSpec(memory_space=ANY)] * 15,
         scratch_shapes=[VMEM(a.shape, a.dtype) for a in (shapes[1], *shapes[4:])]
         + [
-            VMEM((128, 128), f32), VMEM((experts, e_fc1.shape[1], wide), bf), VMEM((16, 32, slim), bf), VMEM((2, 16, 32, slim), bf), VMEM((model, slim), f32),
+            VMEM((128, 128), f32), VMEM((4, 8, 8 * rows + -8 * rows % 128), f32), VMEM((experts, e_fc1.shape[1], wide), bf), VMEM((16, 32, slim), bf), VMEM((2, 16, 32, slim), bf), VMEM((model, slim), f32),
             VMEM((2, model, q_half), bf), VMEM((2, model, o_half), bf), VMEM((2, 4, 2 * rows, a_half // 2), bf),
             VMEM((2, rows, q_half), f32), VMEM((2, rows, o_half), f32), VMEM((2, rows, a_half), f32),
             VMEM((2 * rows, q_half), f32), VMEM((2 * rows, o_half), f32), VMEM((2 * rows, a_half), f32),
             VMEM((2 * rows, q_half), bf), VMEM((2 * rows, o_half), bf),
-            VMEM((4, 2, 8, cond.shape[2]), f32), VMEM((4, 8, a_half // 2), f32), VMEM((3, 8, a_half // 2), f32),
+            VMEM((4, 2, 8, 8 * rows + -8 * rows % 128), f32), VMEM((4, 8, a_half // 2), f32), VMEM((3, 8, a_half // 2), f32),
             DMA((3,)), DMA((3,)), DMA((2, 31)), DMA((2, 16)), DMA((2, 16)), DMA((7,)), DMA((8,)), DMA((8,)), DMA((8,)),
             DMA((15,)), DMA((16,)), DMA((2,)), DMA((1,)), DMA((15,)), DMA((7,)), DMA((4, 2)), DMA((4,)), DMA((4,)), DMA((2, 3)), DMA((2, 4)),
         ],
         compiler_params=pltpu.CompilerParams(collective_id=1, has_side_effects=True, vmem_limit_bytes=62 << 20),
         name="front",
-    )(lengths, tokens, cotangent, routes.T, cond, w_ada, w_qkv, w_out, w_router.T, w_fc1, e_fc1)
+    )(lengths, timesteps, tokens, cotangent, routes.T, waves, w_ada, w_qkv, w_out, w_router.T, w_fc1, e_fc1)
     return result
 
 
@@ -634,10 +650,10 @@
 
 def block_kernel(
     mixed, grad, gates, w1_in, w1s_in, w2_in, w2s_in,
-    sum_branch, sum_back, sum_gc, out1, out1s, out2, out2s,
+    sum_branch, sum_back, sum_gc, near1, far1, out1s, out2, out2s,
     own1, own1s, own2, own2s, X, G, gt, w1, w1s, w2, w2s, act, pre, act_s, pre_s, tile_sum, tile_back,
     p_branch, p_back, p_gc, r_branch, r_back, r_gc, d1, d1s, d2, d2s, from1, from1s, from2, from2s,
-    l_sem, o_sem, g_send, g_recv, send, recv, t_send, t_recv, w_send, w_recv,
+    l_sem, o_sem, g_send, g_recv, send, recv, t_send, t_recv, w_send, w_recv, h_send, h_recv,
 ):
     here = y, z, x, c = place()
     me = chip(y, z, x)
@@ -704,15 +720,12 @@
     gather_second(gathers, 3)
     tile(2, 1)
     back_first(2)
-    back_first(1)
     gather_third(gathers, 3)
     tile(3, 0)
 
-    def back_one(step):
+    def back_one(b, step):
         for scatter in scatters:
-            scatter.one(1, step)
-        for scatter in scatters:
-            scatter.one(0, step)
+            scatter.one(b, step)
 
     def back_two(step):
         for scatter in scatters:
@@ -720,7 +733,7 @@
 
     flat = lambda value: value.reshape(value.shape[0] * value.shape[1], value.shape[2])
     twins = [None] * (2 * experts)
-    leaving = []
+    leaving, homeward = [], []
 
     def leave(source, target):
         leaving.append(pltpu.make_async_copy(source, target, o_sem.at[len(leaving)]))
@@ -739,24 +752,42 @@
         own1[e] = (d1[e, :, c].astype(jnp.float32) + from1[e].astype(jnp.float32)).astype(jnp.bfloat16)
         twins[2 * e + 1].wait()
         own2[e] = d2[e, c].astype(jnp.float32) + from2[e].astype(jnp.float32)
-        leave(own1.at[e], out1.at[e])
         leave(own2.at[e], out2.at[e])
-
-    back_one(2)
+        for i in range(4):
+            leave(own1.at[e, 2 * i + 1 - x], far1.at[e, i])
+        leave(own1.at[e, 2 * z + x], near1.at[e, z])
+
+    def along_home(e):
+        for step in LINE:
+            at = along(z, step)
+            sent = remote(own1.at[e, 2 * at + x], near1.at[e, z], h_send.at[e, step], h_recv.at[e, z], device(y, at, x, c))
+            sent.start()
+            homeward.append(sent)
+
+
+    back_one(1, 2)
     tile(3, 1)
     back_first(3)
+    back_one(0, 2)
     back_two(2)
-    back_one(1)
     weight(0)
-    back_two(1)
+    back_one(1, 3)
+    back_first(1)
+    weight(1)
     home(0)
-    back_first(0)
-    weight(1)
-    back_one(3)
+    back_one(0, 3)
     back_two(3)
     home(1)
+    back_one(1, 1)
+    back_first(0)
     weight(2)
+    back_one(0, 1)
+    along_home(0)
+    along_home(1)
+    back_two(1)
     home(2)
+    back_one(1, 0)
+    along_home(2)
     weight(3)
     d1s[...] = tn(flat(X[...]), flat(pre_s[...])).reshape(d1s.shape)
     d2s[...] = tn(flat(act_s[...]), flat(G[...])).astype(jnp.bfloat16).reshape(d2s.shape)
@@ -765,7 +796,8 @@
     twin1s.start()
     twin2s.start()
     home(3)
-    back_one(0)
+    along_home(3)
+    back_one(0, 0)
     twin1s.wait()
     total = d1s[:, c] + from1s[...]
     own1s[...] = low(jnp.concatenate([total, jnp.zeros((16, own1s.shape[1] - total.shape[1], total.shape[2]), jnp.float32)], axis=1))
@@ -779,6 +811,12 @@
     sum_gc[...] = scatters[2].total()
     for copy in leaving:
         copy.wait()
+    for sent in homeward:
+        sent.wait_send()
+    for e in range(experts):
+        for step in LINE:
+            block = near1.at[e, along(z, step)]
+            remote(block, block, h_send.at[0, 0], h_recv.at[e, along(z, step)], sibling).wait_recv()
     for gather in gathers:
         gather.finish()
     for scatter in scatters:
@@ -799,13 +837,14 @@
             shape((toks, model), f32),
             shape((toks, model), f32),
             shape((8, 128), f32),
-            shape((experts, 8, 2 * rows, wide), bf),
+            shape((experts, 4, 2 * rows, wide), bf),
+            shape((experts, 4, 2 * rows, wide), bf),
             shape((16, 32, slim), bf),
             shape((experts, wide // 2, model), f32),
             shape((slim // 2, model), f32),
         ],
         in_specs=[pl.BlockSpec(memory_space=VMEM)] * 3 + [pl.BlockSpec(memory_space=ANY)] * 4,
-        out_specs=[pl.BlockSpec(memory_space=VMEM)] * 3 + [pl.BlockSpec(memory_space=ANY)] * 4,
+        out_specs=[pl.BlockSpec(memory_space=VMEM)] * 3 + [pl.BlockSpec(memory_space=ANY)] * 5,
         scratch_shapes=[
             VMEM((experts, 8, 2 * rows, wide), bf), VMEM((16, 32, slim), bf), VMEM((experts, wide // 2, model), f32), VMEM((slim // 2, model), f32),
             blocks(model), blocks(model), VMEM((16, 16, 128), bf),
@@ -818,26 +857,25 @@
             VMEM((experts, 2, wide // 2, model), bf), VMEM((2, slim // 2, model), bf),
             VMEM((experts, 8, 2 * rows, wide), bf), VMEM((16, rows, slim), f32),
             VMEM((experts, wide // 2, model), bf), VMEM((slim // 2, model), bf),
-            DMA((7,)), DMA((2 * experts + 2,)), DMA((3, 15)), DMA((3, 16)), DMA((3, 15)), DMA((3, 15)), DMA((2 * experts + 2,)), DMA((2 * experts + 2,)),
-            DMA((2,)), DMA((2,)),
+            DMA((7,)), DMA((6 * experts + 2,)), DMA((3, 15)), DMA((3, 16)), DMA((3, 15)), DMA((3, 15)), DMA((2 * experts + 2,)), DMA((2 * experts + 2,)),
+            DMA((2,)), DMA((2,)), DMA((experts, 4)), DMA((experts, 4)),
         ],
         compiler_params=pltpu.CompilerParams(collective_id=2, has_side_effects=True, vmem_limit_bytes=62 << 20),
         name="block",
     )(mixed, grad, gates, w1, w1s, e_fc2, w_fc2)
 
 
-def rear_kernel(lengths, *refs):
-    incoming, refs = refs[:16], refs[16:]
+def rear_kernel(lengths, steps, waves, *refs):
+    incoming, refs = refs[:15], refs[15:]
     (qkv_in, out_in, part1, part1s, output, d_tokens, d_ada, d_qkv, d_out, d_router, own1, own1s), refs = refs[:12], refs[12:]
-    (sum_branch, sum_back, sum_gc, tokens, cotangent, routes, condition, mod, mixed, attn_in, qkv, probs, attn_low, attn_proj, middle, chance), refs = refs[:16], refs[16:]
-    (square, strip_own, slice_own, q_w, o_w, grad_attn, grad_qkv, grad_mid, o_mine, o_got, q_mine, q_got, part_o, part_a, part_b, got_o, got_a, got_b, fin, mod_tile, all_mod, l_sem, s_send, s_recv, send, recv, g_send, g_recv, g_pair, f_send, f_recv, a_send, a_recv, b_send, b_recv, i_sem) = refs
+    (sum_branch, sum_back, sum_gc, tokens, cotangent, routes, mod, mixed, attn_in, qkv, probs, attn_low, attn_proj, middle, chance), refs = refs[:15], refs[15:]
+    (square, slice_own, q_w, o_w, grad_attn, grad_qkv, grad_mid, o_mine, o_got, q_mine, q_got, part_o, part_a, part_b, got_o, got_a, got_b, fin, mod_tile, all_mod, l_sem, s_send, s_recv, send, recv, g_send, g_recv, g_pair, f_send, f_recv, a_send, a_recv, b_send, b_recv, i_sem) = refs
     here = y, z, x, c = place()
-    me, k = chip(y, z, x), 2 * z + x
+    me = chip(y, z, x)
     sibling = device(y, z, x, 1 - c)
     others = [(dy, dz, dx) for dy in (0, 1) for dz in (0, 1, 2, 3) for dx in (0, 1) if (dy, dz, dx) != (0, 0, 0)]
-    plane = [o for o in others if o[0] == 0]
     spot = lambda dy, dz, dx: (1 - y if dy else y, along(z, dz), 1 - x if dx else x)
-    held = (sum_branch, sum_back, sum_gc, tokens, cotangent, routes, condition, mod, mixed, attn_in, qkv, probs, attn_low, attn_proj, middle, chance)
+    held = (sum_branch, sum_back, sum_gc, tokens, cotangent, routes, mod, mixed, attn_in, qkv, probs, attn_low, attn_proj, middle, chance)
     loads = [pltpu.make_async_copy(a, b, i_sem.at[i]) for i, (a, b) in enumerate(zip(incoming, held))]
     local = [pltpu.make_async_copy(qkv_in, q_w, l_sem.at[0]), pltpu.make_async_copy(out_in, o_w, l_sem.at[1])]
     for copy in loads + local:
@@ -849,19 +887,11 @@
         copy.start()
         started.append(copy)
 
-    wide = part1.shape[3]
-    columns = lambda n: own1.at[:, :, pl.ds(pl.multiple_of(wide * n, 128), wide)]
-    home = [pltpu.make_async_copy(part1.at[:, k], strip_own, l_sem.at[2]), pltpu.make_async_copy(part1s.at[me], slice_own, l_sem.at[3])]
-    for copy in home:
-        copy.start()
-
-    def send_experts(aside):
-        for i, o in enumerate(plane):
-            if o[2] == aside:
-                ty, tz, tx = spot(*o)
-                go(remote(part1.at[:, 2 * tz + tx], columns(k), a_send.at[i], a_recv.at[k], device(ty, tz, tx, c)))
-
-    send_experts(0)
+    home = [pltpu.make_async_copy(part1s.at[me], slice_own, l_sem.at[3])]
+    home[0].start()
+    for step in (0, 1, 2, 3):
+        at = along(z, step)
+        go(remote(part1.at[:, at], own1.at[:, z], a_send.at[step], a_recv.at[z], device(y, at, 1 - x, c)))
     for i, o in enumerate(others):
         go(remote(part1s.at[chip(*spot(*o))], own1s.at[me], b_send.at[i], b_recv.at[me], device(*spot(*o), c)))
 
@@ -890,9 +920,8 @@
     term_router = tn(mixed[...], grad_logits)
     for copy in local + home:
         copy.wait()
-    home = [pltpu.make_async_copy(strip_own, columns(k), l_sem.at[2]), pltpu.make_async_copy(slice_own, own1s.at[me], l_sem.at[3])]
-    for copy in home:
-        copy.start()
+    home = [pltpu.make_async_copy(slice_own, own1s.at[me], l_sem.at[3])]
+    home[0].start()
     grad_mixed = sum_back[...] + nt(grad_logits, o_w[0, :, cut:])
     normed, scale = norm(middle[...])
     per_item(3, grad_mixed)
@@ -945,15 +974,15 @@
             i = 1 + 2 * step + side
             swap_q[step, side] = remote(q_mine.at[1 - c, at, :], q_got.at[at, :], s_send.at[i], s_recv.at[i], sibling)
             swap_q[step, side].start()
-    send_experts(1)
     grad_in = nt(grad_qkv[:, :third], q_w[0]) + nt(grad_qkv[:, third:], q_w[1])
     normed, scale = norm(wide_float(tokens[...]))
     per_item(0, grad_in)
     per_item(1, grad_in * normed)
     d_tokens[...] = grad_mid[...] + norm_back(grad_in * (1.0 + modulation(0, 1)), normed, scale)
-    rows16[12] = wide_float(condition[...])
-    rows16[13] = jnp.zeros((2, model), jnp.float32)
-    mod_tile[...] = low(jnp.concatenate([rows16[i] for i in range(14)], axis=0))
+    column = lax.broadcasted_iota(jnp.int32, (8, model), 1)
+    last = jnp.concatenate([rows16[8 + i] for i in range(4)] + [jnp.zeros((4, model), jnp.float32)], axis=0)
+    last = last + conditions(steps, (8, model), 4, column, model // 2, waves[...])
+    mod_tile[...] = low(jnp.concatenate([rows16[i] for i in range(8)] + [last], axis=0))
 
     slot = lambda n: all_mod.at[n, c]
     spread = Gather(here, False, mod_tile, slot, g_send, g_recv, g_pair)
@@ -977,18 +1006,17 @@
     fold(2)
 
     def turn(at):
-        if at == 0:
+        if at == 1:
             spread.second(0)
             for step in LINE:
                 gather_line([spread], step)
-        elif at == 1:
+        elif at == 2:
             for step in LINE:
                 spread.second(step)
-        elif at == 2:
+        elif at == 3:
             for step in (0,) + LINE:
                 spread.third(step)
             spread.finish()
-        else:
             flat = all_mod[...].reshape(32 * 16, model)
             share_rows = rows // 2
             own = (2 * me + c) * share_rows
@@ -1009,9 +1037,8 @@
     swap = remote(fin.at[c, theirs, :], fin.at[c, theirs, :], f_send, f_recv, sibling)
     swap.start()
 
-    for i, o in enumerate(plane):
-        n = 2 * spot(*o)[1] + spot(*o)[2]
-        remote(columns(n), columns(n), a_send.at[i], a_recv.at[n], sibling).wait_recv()
+    for at in range(4):
+        remote(own1.at[:, at], own1.at[:, at], a_send.at[0], a_recv.at[at], sibling).wait_recv()
     for copy in home:
         copy.wait()
     for i, o in enumerate(others):
@@ -1030,14 +1057,13 @@
     d_router[half:, :] = jnp.zeros((128 - half, 128), jnp.float32)
 
 
-def rear(lengths, sums, tokens, cotangent, routes, condition, saved, qkv_w, out_w, part1, part1s):
+def rear(lengths, timesteps, sums, tokens, cotangent, routes, saved, qkv_w, out_w, part1, part1s):
     bf, f32 = jnp.bfloat16, jnp.float32
     toks, model = tokens.shape
     rows = model // 16
-    experts, _, depth, wide = part1.shape
     q_half, o_half = qkv_w.shape[2], out_w.shape[2]
     a_half = model
-    incoming = (*sums, tokens, cotangent, routes.T, condition, *saved)
+    incoming = (*sums, tokens, cotangent, routes.T, *saved)
     shape = jax.ShapeDtypeStruct
     return pl.pallas_call(
         rear_kernel,
@@ -1048,14 +1074,16 @@
             shape((rows // 2, 2 * q_half), f32),
             shape((rows // 2, model), f32),
             shape((128, 128), f32),
-            shape((experts, depth, 8 * wide), bf),
+            shape(part1.shape, bf),
             shape(part1s.shape, bf),
         ],
-        in_specs=[pl.BlockSpec(memory_space=pltpu.SMEM)] + [pl.BlockSpec(memory_space=ANY)] * 20,
+        in_specs=[pl.BlockSpec(memory_space=pltpu.SMEM)] * 2
+        + [pl.BlockSpec(memory_space=VMEM)]
+        + [pl.BlockSpec(memory_space=ANY)] * 19,
         out_specs=[pl.BlockSpec(memory_space=VMEM)] * 6 + [pl.BlockSpec(memory_space=ANY)] * 2,
         scratch_shapes=[VMEM(a.shape, a.dtype) for a in incoming]
         + [
-            VMEM((128, 128), f32), VMEM((experts, depth, wide), bf), VMEM(part1s.shape[1:], bf), VMEM(qkv_w.shape, bf), VMEM(out_w.shape, bf),
+            VMEM((128, 128), f32), VMEM(part1s.shape[1:], bf), VMEM(qkv_w.shape, bf), VMEM(out_w.shape, bf),
             VMEM((toks, model), bf), VMEM((toks, 3 * model), bf), VMEM((toks, model), f32),
             VMEM((2, model, o_half), bf), VMEM((model, o_half), bf),
             VMEM((2, model, q_half), bf), VMEM((model, q_half), bf),
@@ -1063,17 +1091,17 @@
             VMEM((15, rows, o_half), bf), VMEM((15, rows, a_half), bf), VMEM((15, rows, q_half - a_half), bf),
             VMEM((2, rows, q_half + o_half), f32), VMEM((16, model), bf), VMEM((16, 2, 16, model), bf),
             DMA((4,)), DMA((9,)), DMA((9,)), DMA((3, 15)), DMA((3, 15)), DMA((31,)), DMA((16,)), DMA((16,)), DMA, DMA,
-            DMA((7,)), DMA((8,)), DMA((15,)), DMA((16,)), DMA((16,)),
+            DMA((4,)), DMA((4,)), DMA((15,)), DMA((16,)), DMA((16,)),
         ],
         compiler_params=pltpu.CompilerParams(collective_id=3, has_side_effects=True, vmem_limit_bytes=62 << 20),
         name="rear",
-    )(lengths, *incoming, qkv_w, out_w, part1, part1s)
+    )(lengths, timesteps, frequencies(model)[None], *incoming, qkv_w, out_w, part1, part1s)
 
 
 def finish_kernel(*refs):
-    count = (len(refs) - 4) // 3
-    inputs, outputs, staged = refs[:count], refs[count : 2 * count], refs[2 * count : 3 * count]
-    e1, fc1, sem_in, sem = refs[3 * count :]
+    count = (len(refs) - 3) // 3
+    inputs, outputs, staged = refs[:count], refs[count : 2 * count - 1], refs[2 * count - 1 : 3 * count - 1]
+    e1, fc1, sem_in, sem = refs[3 * count - 1 :]
     loads = [pltpu.make_async_copy(a, b, sem_in.at[i]) for i, (a, b) in enumerate(zip(inputs, staged))]
     stores = []
 
@@ -1083,19 +1111,24 @@
 
     for copy in loads:
         copy.start()
-    low_e1, slices, router = staged[:3]
+    near, far, slices, router = staged[:4]
+    x = place()[2]
+    wide = near.shape[3]
     loads[0].wait()
-    for e in range(low_e1.shape[0]):
-        e1[e] = wide_float(low_e1[e])
+    loads[1].wait()
+    for e in range(near.shape[0]):
+        for at in range(near.shape[1]):
+            e1[e, :, pl.ds(pl.multiple_of(wide * (2 * at + x), 128), wide)] = wide_float(near[e, at])
+            e1[e, :, pl.ds(pl.multiple_of(wide * (2 * at + 1 - x), 128), wide)] = wide_float(far[e, at])
         store(e1.at[e], outputs[0].at[e])
-    for load, source, target in zip(loads[3:], staged[3:], outputs[3:]):
+    for load, source, target in zip(loads[4:], staged[4:], outputs[3:]):
         load.wait()
         store(source, target)
-    loads[1].wait()
     loads[2].wait()
-    slim = slices.shape[2]
+    loads[3].wait()
+    rows, slim = fc1.shape[0], slices.shape[2]
     for n in range(slices.shape[0] // 2):
-        pair = [wide_float(slices[2 * n + i])[: fc1.shape[0]] for i in (0, 1)]
+        pair = [wide_float(slices[2 * n + i])[:rows] for i in (0, 1)]
         fc1[:, 2 * n * slim : 2 * (n + 1) * slim] = jnp.concatenate(pair, axis=1)
     store(fc1, outputs[1])
     outputs[2][...] = router[...].T[: outputs[2].shape[0], : outputs[2].shape[1]]
@@ -1103,23 +1136,25 @@
         copy.wait()
 
 
-def finish(own1, own1s, d_router, *others):
+def finish(near1, far1, own1s, d_router, *others):
     f32 = jnp.float32
-    rows = own1.shape[1] // 2
-    wide = (rows, own1s.shape[0] * own1s.shape[2])
+    experts, _, depth, wide = near1.shape
+    rows = depth // 2
+    e1, fc1 = (experts, depth, 8 * wide), (rows, own1s.shape[0] * own1s.shape[2])
     shape = jax.ShapeDtypeStruct
+    inputs = (near1, far1, own1s, d_router, *others)
     result = pl.pallas_call(
         finish_kernel,
-        out_shape=[shape(own1.shape, f32), shape(wide, f32), shape((8, rows), f32)] + [shape(a.shape, a.dtype) for a in others],
-        in_specs=[pl.BlockSpec(memory_space=ANY)] * (3 + len(others)),
+        out_shape=[shape(e1, f32), shape(fc1, f32), shape((8, rows), f32)] + [shape(a.shape, a.dtype) for a in others],
+        in_specs=[pl.BlockSpec(memory_space=ANY)] * len(inputs),
         out_specs=[pl.BlockSpec(memory_space=ANY)] * 2
         + [pl.BlockSpec(memory_space=VMEM)]
         + [pl.BlockSpec(memory_space=ANY)] * len(others),
-        scratch_shapes=[VMEM(a.shape, a.dtype) for a in (own1, own1s, d_router, *others)]
-        + [VMEM(own1.shape, f32), VMEM(wide, f32), DMA((3 + len(others),)), DMA((8 + len(others),))],
+        scratch_shapes=[VMEM(a.shape, a.dtype) for a in inputs]
+        + [VMEM(e1, f32), VMEM(fc1, f32), DMA((len(inputs),)), DMA((8 + len(others),))],
         compiler_params=pltpu.CompilerParams(vmem_limit_bytes=62 << 20),
         name="finish",
-    )(own1, own1s, d_router, *others)
+    )(*inputs)
     return result[0], result[1], result[2].T, *result[3:]
 
 
@@ -1177,19 +1212,17 @@
 def by_slices(
     tokens, timesteps, lengths, routes, cotangent, w_ada, w_qkv, w_out, w_fc1, w_fc2, w_router, e_fc1, e_fc2
 ):
-    model_width = tokens.shape[1]
-    condition = jax.nn.silu(sinusoid(timesteps, model_width)).astype(jnp.bfloat16)
     (w1, w1s, qkv_w, out_w, mod, mixed, grad, gates, attn_in, qkv, probs, attn_low, attn_proj, middle,
      chance) = front(
-        lengths, tokens, cotangent, routes, condition, w_ada, w_qkv, w_out, w_router, w_fc1, e_fc1
-    )
-    *sums, part1, part1s, d_e2, d_fc2 = block(mixed, grad, gates, w1, w1s, e_fc2, w_fc2)
+        lengths, timesteps, tokens, cotangent, routes, w_ada, w_qkv, w_out, w_router, w_fc1, e_fc1
+    )
+    *sums, near1, far1, part1s, d_e2, d_fc2 = block(mixed, grad, gates, w1, w1s, e_fc2, w_fc2)
     saved = (mod, mixed, attn_in, qkv, probs, attn_low, attn_proj, middle, chance)
     output, d_tokens, d_ada, d_qkv, d_out, d_router, own1, own1s = rear(
-        lengths, sums, tokens, cotangent, routes, condition, saved, qkv_w, out_w, part1, part1s
+        lengths, timesteps, sums, tokens, cotangent, routes, saved, qkv_w, out_w, far1, part1s
     )
     d_e1, d_fc1, d_router, output, d_tokens, d_ada, d_qkv, d_out, d_fc2, d_e2 = finish(
-        own1, own1s, d_router, output, d_tokens, d_ada, d_qkv, d_out, d_fc2, d_e2
+        near1, own1, own1s, d_router, output, d_tokens, d_ada, d_qkv, d_out, d_fc2, d_e2
     )
     return (output, d_tokens, d_ada, d_qkv, d_out, d_fc1, d_fc2, d_router, d_e1, d_e2)
 

time: 273 us -> 255 us (0.934)
  Pallas kernels: 264 us -> 249 us
    pallas_call x1, Pallas kernels: 135 us -> 129 us  [block(): pl.pallas_call(block_kernel, out_shape=[shape((toks, model), f32), shape(...]
    pallas_call x1, Pallas kernels: 58.9 us -> 53.8 us  [rear(): pl.pallas_call(rear_kernel, out_shape=[shape((toks, model), bf), shape((t...]
    pallas_call x1, Pallas kernels: 65 us -> 60.8 us  [front(): pl.pallas_call(front_kernel, out_shape=shapes, in_specs=[pl.BlockSpec(mem...]
where the time goes in v2:
time: 255 us; the launch traced here: 250 us
  Pallas kernels  249 us (98%)
    pallas_call x1, Pallas kernels, block(): pl.pallas_call(block_kernel, out_shape=[shape((toks, model), f32), shape(...  129 us
    pallas_call x1, Pallas kernels, front(): pl.pallas_call(front_kernel, out_shape=shapes, in_specs=[pl.BlockSpec(mem...  60.8 us
    pallas_call x1, Pallas kernels, rear(): pl.pallas_call(rear_kernel, out_shape=[shape((toks, model), bf), shape((t...  53.8 us
    pallas_call x1, Pallas kernels, finish(): pl.pallas_call(finish_kernel, out_shape=[shape(e1, f32), shape(fc1, f32),...  5.78 us

profile of v2, /device:TPU:0, one launch (start us, length us, event | category | flops | bytes accessed | tf_op | source)
XLA Modules:
  0.0 250.5 jit_solution(7508908612301089010)
XLA Ops:
  0.6 60.8 %front.1 = (bf16[4,768,384]{2,1,0:T(8,128)(2,1)}, bf16[768,192]{1,0:T(8,128)(2,1)}, bf16[2,768,1152]{2,1,0:T(8,128)(2,1)}, bf16[2,768,512]{2,1,0:T(8,128)(2,1)},...) custom-call(s32[1,2]{1,0:T(1,128)} %lengths.3, ...), custom_call_target="tpu_custom_call" | custom-call | tf_op jit(solution)/shard_map/front/pallas_call | solution.py:568
  61.4 129.0 %block.1 = (f32[128,768]{1,0:T(8,128)}, f32[128,768]{1,0:T(8,128)}, f32[8,128]{1,0:T(8,128)}, bf16[4,4,48,384]{3,2,1,0:T(8,128)(2,1)}, bf16[4,4,48,384]{3,2,1,0:...) custom-call(bf16[128,768]{1,0:T(8,128)(2,1)} %get-tuple-element.51.mixed.refs_7_, ...), custom_call_target="tpu_custom_call" | custom-call | tf_op jit(solution)/shard_map/block/pallas_call | solution.py:834
  190.4 53.8 %rear.1 = (bf16[128,768]{1,0:T(8,128)(2,1)}, f32[128,768]{1,0:T(8,128)}, f32[24,4608]{1,0:T(8,128)}, f32[24,2304]{1,0:T(8,128)}, f32[24,768]{1,0:T(8,128)}, /*in...) custom-call(s32[1,2]{1,0:T(1,128)} %lengths.3, s32[2]{0:T(128)} %steps.3, ...), custom_call_target="tpu_custom_call" | custom-call | tf_op jit(solution)/shard_map/rear/pallas_call | solution.py:1068
  244.2 5.8 %finish.1 = (f32[4,48,3072]{2,1,0:T(8,128)}, f32[24,3072]{1,0:T(8,128)}, f32[8,24]{1,0:T(8,128)}, bf16[128,768]{1,0:T(8,128)(2,1)}, f32[128,768]{1,0:T(8,128)}, ...) custom-call(bf16[4,4,48,384]{3,2,1,0:T(8,128)(2,1)} %get-tuple-eleme, ...), custom_call_target="tpu_custom_call" | custom-call | tf_op jit(solution)/shard_map/finish/pallas_call | solution.py:1146
